TPU v7x, 32 devices: a whole 2x2x4 slice. The times are simulated.
32 devices in a mesh: wide: 16 (over z, x, core), narrow: 2 (over y).
Axes of the slice: x: 2, y: 2, z: 4, core: 2. Of those that a mesh axis runs over, the one named last changes fastest.
Arguments:
- tokens: bfloat16 [12288, 2048], P(('wide', 'narrow')), may hold values from -6 to 6
- segment_ids: int32 [32, 384], P(('wide', 'narrow')), may hold values from 0 to 5, never falling along the last dimension, each value on 1 to 192 neighbouring positions
- language_ids: int32 [32, 384], P(('wide', 'narrow')), may hold values from 0 to 6
- lang_table: bfloat16 [2048, 7], P(('wide', 'narrow')), may hold values from -3 to 3
- norm1_gain: bfloat16 [2048], P(('wide', 'narrow')), may hold values from 0.5 to 1.5
- norm1_bias: bfloat16 [2048], P(('wide', 'narrow')), may hold values from -1 to 1
- qkv_weight: bfloat16 [6144, 2048], P(('wide', 'narrow')), may hold values from -0.125 to 0.125
- qkv_bias: bfloat16 [6144], P(('wide', 'narrow')), may hold values from -1.5 to 1.5
- out_weight: bfloat16 [2048, 2048], P(('wide', 'narrow')), may hold values from -0.75 to 0.75
- norm2_gain: bfloat16 [2048], P(('wide', 'narrow')), may hold values from 0.5 to 1.5
- norm2_bias: bfloat16 [2048], P(('wide', 'narrow')), may hold values from -1 to 1
- gate_up_weight: bfloat16 [11264, 2048], P(('wide', 'narrow')), may hold values from -0.125 to 0.125
- down_weight: bfloat16 [2048, 5632], P(('wide', 'narrow')), may hold values from -0.078125 to 0.078125
- cotangent: bfloat16 [12288, 2048], P(('wide', 'narrow')), may hold values from -6 to 6
Outputs:
- mixed: bfloat16 [12288, 2048], P(('wide', 'narrow'))
- token_grad: bfloat16 [12288, 2048], P(('wide', 'narrow'))
- lang_grad: float32 [2048, 7], P(('wide', 'narrow'))
- norm1_gain_grad: float32 [2048], P(('wide', 'narrow'))
- norm1_bias_grad: float32 [2048], P(('wide', 'narrow'))
- qkv_weight_grad: float32 [6144, 2048], P(('wide', 'narrow'))
- qkv_bias_grad: float32 [6144], P(('wide', 'narrow'))
- out_weight_grad: float32 [2048, 2048], P(('wide', 'narrow'))
- norm2_gain_grad: float32 [2048], P(('wide', 'narrow'))
- norm2_bias_grad: float32 [2048], P(('wide', 'narrow'))
- gate_up_grad: float32 [11264, 2048], P(('wide', 'narrow'))
- down_grad: float32 [2048, 5632], P(('wide', 'narrow'))
Inputs may be any that keep to these rules, and one draw needn't show every extreme that they name: `segment_ids`: within each packed sequence segment ids start at 0 and never fall; a document has 1 to 192 tokens, one exactly that many.
All inputs are finite; a program needn't handle non-finite values.
Results may differ from a plain program's by a relative error of at most 0.013.
Values may be sent and summed in bfloat16 or wider, within the bound.
No kernel may reach another device: no remote copies, remote signals or barrier semaphores. Data moves between devices by JAX's collectives and lax.ppermute only.
A program may use at most 448 MiB of HBM per device.

v0:
```python
import math

import jax
import jax.numpy as jnp
from jax import lax
from jax.sharding import PartitionSpec as P

D = 2048
H = 32
HD = 64
ROT = 16
FF = 5632
LANGS = 7


NEG_FILL = -1e30
NORM_EPS = 1e-05
THETA_LOG = math.log(10000.0)


def layer_norm(values, gain_vec, bias_vec):
    centre = jnp.mean(values, axis=-1, keepdims=True)
    centred = values - centre
    inv_std = lax.rsqrt(jnp.mean(centred * centred, axis=-1, keepdims=True) + NORM_EPS)
    normed = centred * inv_std
    return (normed * gain_vec.astype(jnp.float32) + bias_vec.astype(jnp.float32), normed, inv_std)


def norm_back(grad_out, normed, inv_std, gain_vec):
    scaled = grad_out * gain_vec.astype(jnp.float32)
    inner = (
        scaled
        - jnp.mean(scaled, axis=-1, keepdims=True)
        - normed * jnp.mean(scaled * normed, axis=-1, keepdims=True)
    )
    return (inv_std * inner, jnp.sum(grad_out * normed, axis=0), jnp.sum(grad_out, axis=0))


def rotary_tables(segment_row):
    count_tok = segment_row.shape[0]
    earlier = jnp.sum((segment_row[None, :] < segment_row[:, None]).astype(jnp.int32), axis=1)
    places = (jnp.arange(count_tok, dtype=jnp.int32) - earlier).astype(jnp.float32)
    frequency = jnp.exp(jnp.arange(ROT // 2, dtype=jnp.float32) * (-2.0 * THETA_LOG / ROT))
    angles = places[:, None] * frequency[None, :]
    return (jnp.cos(angles), jnp.sin(angles))


def rotate(field, cosine, sine_tab, sign_val):
    half_rot = ROT // 2
    first_half = field[..., :half_rot]
    second_half = field[..., half_rot:ROT]
    cos_b = cosine[:, None, :]
    sin_b = sign_val * sine_tab[:, None, :]
    return jnp.concatenate(
        [
            first_half * cos_b - second_half * sin_b,
            second_half * cos_b + first_half * sin_b,
            field[..., ROT:],
        ],
        axis=-1,
    )


def mul_rows(left, weight):
    return lax.dot_general(
        left, weight, (((1,), (1,)), ((), ())), preferred_element_type=jnp.float32
    )


def weight_grad(grad_rows, inputs):
    return lax.dot_general(
        grad_rows, inputs, (((0,), (0,)), ((), ())), preferred_element_type=jnp.float32
    )


def heads_first(field, group_size):
    count_tok = field.shape[0]
    return jnp.transpose(field.reshape(count_tok, H, HD), (1, 0, 2)).reshape(
        H // group_size, group_size, count_tok, HD
    )


def tokens_first(field):
    count_tok = field.shape[2]
    return jnp.transpose(field.reshape(H, count_tok, HD), (1, 0, 2)).reshape(count_tok, D)


def ffn_weights(gate_up_weight, down_weight):
    gathered = (
        lax.all_gather(gate_up_weight, ("wide", "narrow"), axis=0, tiled=True),
        lax.all_gather(down_weight, ("wide", "narrow"), axis=0, tiled=True),
    )
    return gathered


def swiglu_back(grad_hidden, gate_part, up_part, sigma_gate, silu_gate):
    grad_gate = grad_hidden * up_part * (sigma_gate + gate_part * sigma_gate * (1.0 - sigma_gate))
    return jnp.concatenate([grad_gate, grad_hidden * silu_gate], axis=1).astype(jnp.bfloat16)


def per_device(
    tokens,
    segment_ids,
    language_ids,
    lang_table,
    norm1_gain,
    norm1_bias,
    qkv_weight,
    qkv_bias,
    out_weight,
    norm2_gain,
    norm2_bias,
    gate_up_weight,
    down_weight,
    cotangent,
):
    attn_set = (
        lax.all_gather(lang_table, ("wide", "narrow"), axis=0, tiled=True),
        lax.all_gather(norm1_gain, ("wide", "narrow"), axis=0, tiled=True),
        lax.all_gather(norm1_bias, ("wide", "narrow"), axis=0, tiled=True),
        lax.all_gather(qkv_weight, ("wide", "narrow"), axis=0, tiled=True),
        lax.all_gather(qkv_bias, ("wide", "narrow"), axis=0, tiled=True),
        lax.all_gather(out_weight, ("wide", "narrow"), axis=0, tiled=True),
        lax.all_gather(norm2_gain, ("wide", "narrow"), axis=0, tiled=True),
        lax.all_gather(norm2_bias, ("wide", "narrow"), axis=0, tiled=True),
    )
    count_tok = tokens.shape[0]
    group_size = math.gcd(H, 8)
    score_scale = 1.0 / math.sqrt(HD)
    segment_row = segment_ids[0]
    language_row = language_ids[0]
    cosine, sine_tab = rotary_tables(segment_row)
    positions = jnp.arange(count_tok, dtype=jnp.int32)
    allowed = (segment_row[:, None] == segment_row[None, :]) & (
        positions[None, :] <= positions[:, None]
    )
    one_hot = language_row[:, None] == jnp.arange(LANGS, dtype=jnp.int32)[None, :]

    def masked_scores(query_g, key_g):
        scores = (
            jnp.einsum("hqd,hkd->hqk", query_g, key_g, preferred_element_type=jnp.float32)
            * score_scale
        )
        return jnp.where(allowed[None], scores, NEG_FILL)

    def attend(group_items):
        query_g, key_g, value_g = group_items
        scores = masked_scores(query_g, key_g)
        row_max = jnp.max(scores, axis=-1, keepdims=True)
        unnormed = jnp.exp(scores - row_max)
        row_total = jnp.sum(unnormed, axis=-1, keepdims=True)
        attn_probs = (unnormed / row_total).astype(jnp.bfloat16)
        result = jnp.einsum("hqk,hkd->hqd", attn_probs, value_g, preferred_element_type=jnp.float32)
        return (result.astype(jnp.bfloat16), (row_max + jnp.log(row_total))[..., 0])

    def attend_back(group_items):
        query_g, key_g, value_g, grad_g, log_total = group_items
        scores = masked_scores(query_g, key_g)
        attn_probs = jnp.exp(scores - log_total[..., None])
        grad_probs = jnp.einsum("hqd,hkd->hqk", grad_g, value_g, preferred_element_type=jnp.float32)
        row_dot = jnp.sum(attn_probs * grad_probs, axis=-1, keepdims=True)
        grad_scores = (attn_probs * (grad_probs - row_dot)).astype(jnp.bfloat16)
        grad_value = jnp.einsum(
            "hqk,hqd->hkd",
            attn_probs.astype(jnp.bfloat16),
            grad_g,
            preferred_element_type=jnp.float32,
        )
        grad_query = (
            jnp.einsum("hqk,hkd->hqd", grad_scores, key_g, preferred_element_type=jnp.float32)
            * score_scale
        )
        grad_key = (
            jnp.einsum("hqk,hqd->hkd", grad_scores, query_g, preferred_element_type=jnp.float32)
            * score_scale
        )
        return (grad_query, grad_key, grad_value)

    stream0 = tokens.astype(jnp.float32) + jnp.dot(
        one_hot.astype(jnp.bfloat16), attn_set[0].T, preferred_element_type=jnp.float32
    )
    normed_in, norm1_hat, norm1_inv = layer_norm(stream0, attn_set[1], attn_set[2])
    normed_in = normed_in.astype(jnp.bfloat16)
    projected = mul_rows(normed_in, attn_set[3]) + attn_set[4].astype(jnp.float32)
    query = rotate(projected[:, :D].reshape(count_tok, H, HD), cosine, sine_tab, 1.0).astype(
        jnp.bfloat16
    )
    key_rot = rotate(
        projected[:, D : 2 * D].reshape(count_tok, H, HD), cosine, sine_tab, 1.0
    ).astype(jnp.bfloat16)
    value_in = projected[:, 2 * D :].astype(jnp.bfloat16)
    query_grp = heads_first(query, group_size)
    key_grp = heads_first(key_rot, group_size)
    value_grp = heads_first(value_in, group_size)
    attended_grp, log_totals = lax.map(attend, (query_grp, key_grp, value_grp))
    attended = tokens_first(attended_grp)
    stream1 = stream0 + mul_rows(attended, attn_set[5])
    normed_mid, norm2_hat, norm2_inv = layer_norm(stream1, attn_set[6], attn_set[7])
    normed_mid = normed_mid.astype(jnp.bfloat16)
    mlp_set = ffn_weights(gate_up_weight, down_weight)
    gate_up = mul_rows(normed_mid, mlp_set[0])
    gate_part = gate_up[:, :FF]
    up_part = gate_up[:, FF:]
    sigma_gate = jax.nn.sigmoid(gate_part)
    silu_gate = gate_part * sigma_gate
    hidden = (silu_gate * up_part).astype(jnp.bfloat16)
    mixed = (stream1 + mul_rows(hidden, mlp_set[1])).astype(jnp.bfloat16)
    attn_back = (
        lax.all_gather(lang_table, ("wide", "narrow"), axis=0, tiled=True),
        lax.all_gather(norm1_gain, ("wide", "narrow"), axis=0, tiled=True),
        lax.all_gather(norm1_bias, ("wide", "narrow"), axis=0, tiled=True),
        lax.all_gather(qkv_weight, ("wide", "narrow"), axis=0, tiled=True),
        lax.all_gather(qkv_bias, ("wide", "narrow"), axis=0, tiled=True),
        lax.all_gather(out_weight, ("wide", "narrow"), axis=0, tiled=True),
        lax.all_gather(norm2_gain, ("wide", "narrow"), axis=0, tiled=True),
        lax.all_gather(norm2_bias, ("wide", "narrow"), axis=0, tiled=True),
    )
    mlp_back = ffn_weights(gate_up_weight, down_weight)
    down_sum = lax.psum_scatter(
        weight_grad(cotangent, hidden), ("wide", "narrow"), scatter_dimension=0, tiled=True
    )
    grad_hidden = jnp.dot(cotangent, mlp_back[1], preferred_element_type=jnp.float32)
    grad_gu = swiglu_back(grad_hidden, gate_part, up_part, sigma_gate, silu_gate)
    gate_up_sum = lax.psum_scatter(
        weight_grad(grad_gu, normed_mid), ("wide", "narrow"), scatter_dimension=0, tiled=True
    )
    grad_mid = jnp.dot(grad_gu, mlp_back[0], preferred_element_type=jnp.float32)
    grad_norm2, gain2_grad, bias2_grad = norm_back(grad_mid, norm2_hat, norm2_inv, attn_back[6])
    grad_stream1 = cotangent.astype(jnp.float32) + grad_norm2
    grad_attn = grad_stream1.astype(jnp.bfloat16)
    out_grad = weight_grad(grad_attn, attended)
    grad_attended = jnp.dot(grad_attn, attn_back[5], preferred_element_type=jnp.float32).astype(
        jnp.bfloat16
    )
    grad_q, grad_k, grad_v = lax.map(
        attend_back,
        (query_grp, key_grp, value_grp, heads_first(grad_attended, group_size), log_totals),
    )
    grad_q = rotate(tokens_first(grad_q).reshape(count_tok, H, HD), cosine, sine_tab, -1.0).reshape(
        count_tok, D
    )
    grad_k = rotate(tokens_first(grad_k).reshape(count_tok, H, HD), cosine, sine_tab, -1.0).reshape(
        count_tok, D
    )
    grad_proj = jnp.concatenate([grad_q, grad_k, tokens_first(grad_v)], axis=1).astype(jnp.bfloat16)
    qkv_grad = weight_grad(grad_proj, normed_in)
    qkv_bias_grad = jnp.sum(grad_proj.astype(jnp.float32), axis=0)
    grad_in = jnp.dot(grad_proj, attn_back[3], preferred_element_type=jnp.float32)
    grad_norm1, gain1_grad, bias1_grad = norm_back(grad_in, norm1_hat, norm1_inv, attn_back[1])
    grad_stream0 = grad_stream1 + grad_norm1
    lang_grad = lax.dot_general(
        grad_stream0,
        one_hot.astype(jnp.float32),
        (((0,), (0,)), ((), ())),
        precision=lax.Precision.HIGHEST,
    )
    attn_sums = (
        lax.psum_scatter(lang_grad, ("wide", "narrow"), scatter_dimension=0, tiled=True),
        lax.psum_scatter(gain1_grad, ("wide", "narrow"), scatter_dimension=0, tiled=True),
        lax.psum_scatter(bias1_grad, ("wide", "narrow"), scatter_dimension=0, tiled=True),
        lax.psum_scatter(qkv_grad, ("wide", "narrow"), scatter_dimension=0, tiled=True),
        lax.psum_scatter(qkv_bias_grad, ("wide", "narrow"), scatter_dimension=0, tiled=True),
        lax.psum_scatter(out_grad, ("wide", "narrow"), scatter_dimension=0, tiled=True),
        lax.psum_scatter(gain2_grad, ("wide", "narrow"), scatter_dimension=0, tiled=True),
        lax.psum_scatter(bias2_grad, ("wide", "narrow"), scatter_dimension=0, tiled=True),
    )
    return (
        mixed,
        grad_stream0.astype(jnp.bfloat16),
        attn_sums[0],
        attn_sums[1],
        attn_sums[2],
        attn_sums[3],
        attn_sums[4],
        attn_sums[5],
        attn_sums[6],
        attn_sums[7],
        gate_up_sum,
        down_sum,
    )


def solution(mesh):
    placed = (
        P(("wide", "narrow"), None),
        P(("wide", "narrow"), None),
        P(("wide", "narrow"), None),
        P(("wide", "narrow"), None),
        P(("wide", "narrow")),
        P(("wide", "narrow")),
        P(("wide", "narrow"), None),
        P(("wide", "narrow")),
        P(("wide", "narrow"), None),
        P(("wide", "narrow")),
        P(("wide", "narrow")),
        P(("wide", "narrow"), None),
        P(("wide", "narrow"), None),
        P(("wide", "narrow"), None),
    )
    return jax.shard_map(
        per_device,
        mesh=mesh,
        in_specs=placed,
        out_specs=(
            P(("wide", "narrow"), None),
            P(("wide", "narrow"), None),
            P(("wide", "narrow"), None),
            P(("wide", "narrow")),
            P(("wide", "narrow")),
            P(("wide", "narrow"), None),
            P(("wide", "narrow")),
            P(("wide", "narrow"), None),
            P(("wide", "narrow")),
            P(("wide", "narrow")),
            P(("wide", "narrow"), None),
            P(("wide", "narrow"), None),
        ),
        check_vma=False,
    )
```

profile of v0, /device:TPU:13, one launch (start us, length us, event | category | flops | bytes accessed | tf_op | source)
XLA Modules:
  0.0 4628.8 jit_solution(9365297763846219820)
XLA Ops:
  10.2 49.9 %all-gather = bf16[32,64,7]{1,2,0:T(8,128)(2,1)S(1)} all-gather(bf16[1,64,7]{1,2,0:T(8,128)(2,1)S(1)} %bitcast.175), channel_id=1, replica_groups=mesh['wide'=16,'narrow'=2] {'wide','narrow'}, dimensions={0}, use_global_device_ids=true | all-gather | bytes 29568 | tf_op jit(solution)/shard_map/all_gather | solution.py:118
  61.5 62.9 %all-reduce.11 = (bf16[6144]{0:T(1024)(128)(2,1)S(1)}, bf16[2048]{0:T(1024)(128)(2,1)S(1)}, bf16[2048]{0:T(1024)(128)(2,1)S(1)}, bf16[2048]{0:T(1024)(128)(2,1)S(1)}, bf16[2048]{0:T(1024)(128)(2,1)S(1)}) all-reduce(bf16[6144]{0:T(1024)(128)(2,1)S(1)} %dynamic-update-slice.2, ...), channel_id=1, replica_groups=mesh['wide'=16,'narrow'=2] {'wide','narrow'}, use_global_device_ids=true, to_apply=%add.2 | all-reduce | flops 14336 | bytes 57344
  128.5 37.8 all-gather.6.cloned.1.call-done
  166.4 16.7 convolution_add_fusion
  186.4 6.3 fusion.74
  192.7 3.5 copy.63
  199.0 3.6 copy.64
  212.3 25.8 while.28
  238.1 8.8 all-gather.8.cloned.1.call-done
  247.0 6.7 fusion.76
  255.8 246.0 %all-gather.10.cloned.1.call-done = bf16[11264,2048]{1,0:T(8,128)(2,1)} async-done(((bf16[352,2048]{1,0:T(8,128)(2,1)}), bf16[11264,2048]{1,0:T(8,128)(2,1)}) %all-gather.10.cloned.1.call-update) | async-done | bytes 46137360 | tf_op jit(solution)/shard_map/all_gather | solution.py:90
  501.8 28.6 fusion.72
  530.5 117.1 %all-gather.12.cloned.1.call-done = bf16[2048,5632]{1,0:T(8,128)(2,1)} async-done(((bf16[64,5632]{1,0:T(8,128)(2,1)}), bf16[2048,5632]{1,0:T(8,128)(2,1)}) %all-gather.12.cloned.1.call-update) | async-done | bytes 23068688 | tf_op jit(solution)/shard_map/all_gather | solution.py:91
  647.5 22.2 multiply_convert_fusion.2
  669.8 28.1 multiply_reduce_fusion.1
  702.8 7.9 convolution_convert_fusion
  713.5 43.9 while.29
  765.6 18.6 multiply_reduce_fusion.2
  784.1 4.2 fusion.73
  788.4 3.7 fusion.65
  792.4 12.8 fusion.62
  805.9 22.4 fusion.70
  829.7 20.6 convolution_bitcast_fusion
  850.3 42.4 copy.74
  894.5 37.3 fusion.60
  931.9 3.8 convert_reduce_fusion
  935.7 42.4 all-reduce.10
  981.1 15.8 add_convert_fusion
  998.3 285.4 %reduce-scatter.12.cloned.1.call-done = f32[64,2048]{1,0:T(8,128)} async-done(((f32[2048,2048]{1,0:T(8,128)}), f32[64,2048]{1,0:T(8,128)}) %reduce-scatter.12.cloned.1.call-update) | async-done | bytes 524304 | tf_op jit(solution)/shard_map/reduce_scatter | solution.py:263
  1283.8 439.0 %reduce-scatter.10.cloned.1.call-done = f32[192,2048]{1,0:T(8,128)} async-done(((f32[6144,2048]{1,0:T(8,128)}), f32[192,2048]{1,0:T(8,128)}) %reduce-scatter.10.cloned.1.call-update) | async-done | bytes 1572880 | tf_op jit(solution)/shard_map/reduce_scatter | solution.py:261
  1722.7 969.8 %reduce-scatter.18.cloned.1.call-done = f32[64,5632]{1,0:T(8,128)} async-done(((f32[2048,5632]{1,0:T(8,128)}), f32[64,5632]{1,0:T(8,128)}) %reduce-scatter.18.cloned.1.call-update) | async-done | bytes 1441808
  2692.6 1929.2 %reduce-scatter.14.cloned.1.call-done = f32[352,2048]{1,0:T(8,128)} async-done(((f32[11264,2048]{1,0:T(8,128)}), f32[352,2048]{1,0:T(8,128)}) %reduce-scatter.14.cloned.1.call-update) | async-done | bytes 2883600 | tf_op jit(solution)/shard_map/reduce_scatter | solution.py:224
  (245 shorter events, 119.7 us)
Async XLA Ops:
  7.2 53.0 %copy-start.42 = (s32[1,384]{1,0:T(1,128)S(1)}, s32[1,384]{1,0:T(1,128)}, u32[]{:S(2)}) copy-start(s32[1,384]{1,0:T(1,128)} %param.20) | copy-start | bytes 4612
  7.2 53.0 %copy-start.44 = (bf16[64]{0:T(256)(128)(2,1)S(1)}, bf16[64]{0:T(256)(128)(2,1)}, u32[]{:S(2)}) copy-start(bf16[64]{0:T(256)(128)(2,1)} %param.23) | copy-start | bytes 388
  7.2 53.3 %copy-start.45 = (bf16[64]{0:T(256)(128)(2,1)S(1)}, bf16[64]{0:T(256)(128)(2,1)}, u32[]{:S(2)}) copy-start(bf16[64]{0:T(256)(128)(2,1)} %param.22) | copy-start | bytes 388
  7.2 53.5 %copy-start.46 = (bf16[64]{0:T(256)(128)(2,1)S(1)}, bf16[64]{0:T(256)(128)(2,1)}, u32[]{:S(2)}) copy-start(bf16[64]{0:T(256)(128)(2,1)} %param.28) | copy-start | bytes 388
  7.2 53.8 %copy-start.47 = (bf16[64]{0:T(256)(128)(2,1)S(1)}, bf16[64]{0:T(256)(128)(2,1)}, u32[]{:S(2)}) copy-start(bf16[64]{0:T(256)(128)(2,1)} %param.27) | copy-start | bytes 388
  7.2 54.0 %copy-start.48 = (bf16[192]{0:T(256)(128)(2,1)S(1)}, bf16[192]{0:T(256)(128)(2,1)}, u32[]{:S(2)}) copy-start(bf16[192]{0:T(256)(128)(2,1)} %param.25) | copy-start | bytes 1156
  7.3 117.2 %copy-start.43 = (s32[1,384]{1,0:T(1,128)S(1)}, s32[1,384]{1,0:T(1,128)}, u32[]{:S(2)}) copy-start(s32[1,384]{1,0:T(1,128)} %param.19) | copy-start | bytes 4612
  7.3 159.1 %all-gather.6.cloned.1.call-start = ((), (), s32[]{:S(2)}) async-start(), calls=%async_computation.5 | async-start | bytes 25952256 | tf_op jit(solution)/shard_map/all_gather | solution.py:121
  8.0 239.0 %all-gather.8.cloned.1.call-start = ((), (), s32[]{:S(2)}) async-start(), calls=%async_computation.6 | async-start | bytes 8650752 | tf_op jit(solution)/shard_map/all_gather | solution.py:123
  8.7 493.1 %all-gather.10.cloned.1.call-start = ((), (), s32[]{:S(2)}) async-start(), calls=%async_computation.7 | async-start | bytes 47579136 | tf_op jit(solution)/shard_map/all_gather | solution.py:90
  9.5 638.1 %all-gather.12.cloned.1.call-start = ((), (), s32[]{:S(2)}) async-start(), calls=%async_computation.8 | async-start | bytes 23789568 | tf_op jit(solution)/shard_map/all_gather | solution.py:91
  10.1 986.8 %reduce-scatter.16.cloned.1.call-start = ((), (), s32[]{:S(2)}) async-start(), calls=%async_computation.12 | async-start | bytes 1081344
  60.2 67.2 %copy-start.31 = (s32[384]{0:T(512)}, s32[384]{0:T(512)S(1)}, u32[]{:S(2)}) copy-start(s32[384]{0:T(512)S(1)} %reduce) | copy-start | bytes 4612
  124.4 41.9 copy-start.27
  124.5 41.9 copy-start.18
  124.5 377.3 %copy-start.25 = (f32[2048]{0:T(1024)}, f32[2048]{0:T(1024)S(1)}, u32[]{:S(2)}) copy-start(f32[2048]{0:T(1024)S(1)} %convert_element_type.84) | copy-start | bytes 24580
  124.5 573.4 %copy-start.20 = (f32[2048]{0:T(1024)}, f32[2048]{0:T(1024)S(1)}, u32[]{:S(2)}) copy-start(f32[2048]{0:T(1024)S(1)} %convert_element_type.83) | copy-start | bytes 24580
  126.9 120.1 %copy-start = (f32[384,2048]{1,0:T(8,128)}, f32[384,2048]{1,0:T(8,128)S(1)}, u32[]{:S(2)}) copy-start(f32[384,2048]{1,0:T(8,128)S(1)} %get-tuple-element.276) | copy-start | bytes 9437188
  126.9 56.2 %copy-start.23 = (f32[384]{0:T(512)}, f32[384]{0:T(512)S(1)}, u32[]{:S(2)}) copy-start(f32[384]{0:T(512)S(1)} %broadcast_multiply_fusion.6) | copy-start | bytes 4612
  127.4 55.7 %copy-start.33 = (f32[384]{0:T(512)}, f32[384]{0:T(512)S(1)}, u32[]{:S(2)}) copy-start(f32[384]{0:T(512)S(1)} %add_rsqrt_fusion.1) | copy-start | bytes 4612
  128.5 79.4 %copy-start.16 = (f32[384,8]{0,1:T(8,128)}, f32[384,8]{0,1:T(8,128)S(1)}, u32[]{:S(2)}) copy-start(f32[384,8]{0,1:T(8,128)S(1)} %get-tuple-element.274) | copy-start | bytes 36868
  253.7 444.2 %copy-start.29 = (f32[384]{0:T(512)}, f32[384]{0:T(512)S(1)}, u32[]{:S(2)}) copy-start(f32[384]{0:T(512)S(1)} %broadcast_multiply_fusion.5) | copy-start | bytes 4612
  255.8 442.1 %copy-start.35 = (f32[384]{0:T(512)}, f32[384]{0:T(512)S(1)}, u32[]{:S(2)}) copy-start(f32[384]{0:T(512)S(1)} %add_rsqrt_fusion) | copy-start | bytes 4612
  530.5 139.3 %copy-start.7 = (f32[384,2048]{1,0:T(8,128)S(1)}, f32[384,2048]{1,0:T(8,128)}, u32[]{:S(2)}) copy-start(f32[384,2048]{1,0:T(8,128)} %copy-done.6) | copy-start | bytes 9437188
  669.8 28.2 copy-start.12
  765.5 18.6 copy-start.5
  784.1 4.2 copy-start.32
  792.1 491.6 %reduce-scatter.12.cloned.1.call-start = ((), (), s32[]{:S(2)}) async-start(), calls=%async_computation.10 | async-start | bytes 17301504 | tf_op jit(solution)/shard_map/reduce_scatter | solution.py:263
  805.2 917.6 %reduce-scatter.10.cloned.1.call-start = ((), (), s32[]{:S(2)}) async-start(), calls=%async_computation.9 | async-start | bytes 51904512 | tf_op jit(solution)/shard_map/reduce_scatter | solution.py:261
  828.3 1864.3 %reduce-scatter.18.cloned.1.call-start = ((), (), s32[]{:S(2)}) async-start(), calls=%async_computation.13 | async-start | bytes 47579136
  892.7 3729.2 %reduce-scatter.14.cloned.1.call-start = ((), (), s32[]{:S(2)}) async-start(), calls=%async_computation.11 | async-start | bytes 95158272 | tf_op jit(solution)/shard_map/reduce_scatter | solution.py:224
  931.8 3.8 copy-start.37
  (35 other events, 80.7 us)
Sparse Core Ops, SparseCore 0:
  11.0 155.3 all-gather.5
  169.5 77.4 all-gather.7
  249.8 251.9 all-gather.9
  504.6 142.9 all-gather.11
  792.2 113.8 reduce-scatter.15
  909.0 374.7 reduce-scatter.11
  1291.9 430.8 reduce-scatter.9
  1725.7 966.8 reduce-scatter.17
  2695.6 1926.1 reduce-scatter.13
where the time goes:
time: 4640 us; the launch traced here: 4630 us
  waiting for transfers between devices  4040 us (87%)
  matrix products  297 us (6%)
  blocking collectives  155 us (3%)
  local copies, waits for them, and re-layouts  93.1 us (2%)
    reduce_scatter x1, waiting for transfers between devices, per_device(): lax.psum_scatter(weight_grad(grad_gu, normed_mid), ('wide', 'narrow'), sc...  1930 us
    unnamed x11, waiting for transfers between devices  973 us
    reduce_scatter x1, waiting for transfers between devices, per_device(): lax.psum_scatter(qkv_grad, ('wide', 'narrow'), scatter_dimension=0, tiled...  439 us
    reduce_scatter x1, waiting for transfers between devices, per_device(): lax.psum_scatter(out_grad, ('wide', 'narrow'), scatter_dimension=0, tiled...  285 us
    all_gather x1, waiting for transfers between devices, ffn_weights(): lax.all_gather(gate_up_weight, ('wide', 'narrow'), axis=0, tiled=True)  246 us
    all_gather x1, waiting for transfers between devices, ffn_weights(): lax.all_gather(down_weight, ('wide', 'narrow'), axis=0, tiled=True)  117 us
    unnamed x2, blocking collectives  105 us
    dot_general x4, matrix products, weight_grad(): lax.dot_general(grad_rows, inputs, (((0,), (0,)), ((), ())), preferred_el...  93.1 us
  transfers between devices with their start and end apart: 9, of which 8 were waited for; matrix products, arithmetic and copies ran while one was open for 6% of the time, Pallas kernels for 0%

commit v1 on v0

v1 whole, which is shorter than its diff:
```python
import functools
import math

import jax
import jax.numpy as jnp
from jax import lax
from jax.experimental import pallas as pl
from jax.experimental.pallas import tpu as pltpu
from jax.sharding import PartitionSpec as P

D = 2048
H = 32
HD = 64
ROT = 16
FF = 5632
LANGS = 7

NEG_FILL = -1e30
NORM_EPS = 1e-05
THETA_LOG = math.log(10000.0)
AXES = ("wide", "narrow")
BF = jnp.bfloat16
F32 = jnp.float32
HEADS_STEP = 4
LANES = HEADS_STEP * HD
Q_BLOCK = 128
SMALL_ROWS = LANGS + 4 + 3
SHORT = pl.CostEstimate(flops=1, bytes_accessed=1, transcendentals=0)


def layer_norm(values, gain_vec, bias_vec):
    centre = jnp.mean(values, axis=-1, keepdims=True)
    centred = values - centre
    inv_std = lax.rsqrt(jnp.mean(centred * centred, axis=-1, keepdims=True) + NORM_EPS)
    normed = centred * inv_std
    return (normed * gain_vec.astype(F32) + bias_vec.astype(F32), normed, inv_std)


def norm_back(grad_out, normed, inv_std, gain_vec):
    scaled = grad_out * gain_vec.astype(F32)
    inner = (
        scaled
        - jnp.mean(scaled, axis=-1, keepdims=True)
        - normed * jnp.mean(scaled * normed, axis=-1, keepdims=True)
    )
    return (inv_std * inner, jnp.sum(grad_out * normed, axis=0), jnp.sum(grad_out, axis=0))


def rotary_tables(segment_row):
    count_tok = segment_row.shape[0]
    earlier = jnp.sum((segment_row[None, :] < segment_row[:, None]).astype(jnp.int32), axis=1)
    places = (jnp.arange(count_tok, dtype=jnp.int32) - earlier).astype(F32)
    frequency = jnp.exp(jnp.arange(ROT // 2, dtype=F32) * (-2.0 * THETA_LOG / ROT))
    angles = places[:, None] * frequency[None, :]
    cosine, sine = jnp.cos(angles), jnp.sin(angles)
    rest = HD - ROT
    half = jnp.zeros((count_tok, ROT // 2), F32)
    none = jnp.zeros((count_tok, rest), F32)
    cos_head = jnp.concatenate([cosine, cosine, none + 1.0], axis=1)
    first_head = jnp.concatenate([-sine, half, none], axis=1)
    second_head = jnp.concatenate([half, sine, none], axis=1)
    return tuple(jnp.tile(t, (1, HEADS_STEP)) for t in (cos_head, first_head, second_head))


def mul_rows(left, weight):
    return lax.dot_general(left, weight, (((1,), (1,)), ((), ())), preferred_element_type=F32)


def weight_grad(grad_rows, inputs):
    return lax.dot_general(grad_rows, inputs, (((0,), (0,)), ((), ())), preferred_element_type=F32)


def shifts(field):
    half = ROT // 2
    return (pltpu.roll(field, LANES - half, 1), pltpu.roll(field, half, 1))


def lane_masks(scale):
    head_of = lax.broadcasted_iota(jnp.int32, (1, LANES), 1) // HD
    return [jnp.where(head_of == head, scale, 0.0).astype(BF) for head in range(HEADS_STEP)]


def by_head(rows, masks):
    return jnp.concatenate([rows * mask for mask in masks], axis=0)


def joined(field, masks):
    parts = jnp.split(field, HEADS_STEP, axis=0)
    return sum(part * mask.astype(F32) for part, mask in zip(parts, masks))


def probs_of(queries, keys, allowed):
    scores = jnp.where(allowed, mul_rows(keys, queries), NEG_FILL)
    unnormed = jnp.exp(scores - jnp.max(scores, axis=0, keepdims=True))
    return unnormed * (1.0 / jnp.sum(unnormed, axis=0, keepdims=True))


def allowed_of(seg_col, seg_row, block):
    start, end = block * Q_BLOCK, (block + 1) * Q_BLOCK
    key_at = lax.broadcasted_iota(jnp.int32, (end, Q_BLOCK), 0)
    query_at = lax.broadcasted_iota(jnp.int32, (end, Q_BLOCK), 1) + start
    one = (seg_col[:end, :] == seg_row[:, start:end]) & (key_at <= query_at)
    return jnp.concatenate([one] * HEADS_STEP, axis=1)


def attend_kernel(
    x_ref, wq_ref, wk_ref, wv_ref, bq_ref, bk_ref, bv_ref, cos_ref, first_ref, second_ref,
    segc_ref, segr_ref, q_ref, k_ref, v_ref, out_ref,
):
    x_in = x_ref[...]
    cosine, first, second = cos_ref[...], first_ref[...], second_ref[...]

    def turned(w_ref, b_ref):
        field = mul_rows(x_in, w_ref[...]) + b_ref[...]
        ahead, behind = shifts(field)
        return (field * cosine + ahead * first + behind * second).astype(BF)

    q_ref[...] = turned(wq_ref, bq_ref)
    k_ref[...] = turned(wk_ref, bk_ref)
    v_ref[...] = (mul_rows(x_in, wv_ref[...]) + bv_ref[...]).astype(BF)
    scaled, masks = lane_masks(1.0 / math.sqrt(HD)), lane_masks(1.0)
    seg_col, seg_row = segc_ref[...], segr_ref[...]
    for block in range(x_in.shape[0] // Q_BLOCK):
        start, end = block * Q_BLOCK, (block + 1) * Q_BLOCK
        queries = by_head(q_ref[start:end, :], scaled)
        probs = probs_of(queries, k_ref[:end, :], allowed_of(seg_col, seg_row, block))
        out_ref[start:end, :] = joined(weight_grad(probs.astype(BF), v_ref[:end, :]), masks).astype(BF)


def attend_back_kernel(
    q_ref, k_ref, v_ref, g_ref, cos_ref, first_ref, second_ref, segc_ref, segr_ref, *rest
):
    grad_ref, dk_sum, dv_sum = rest[-3:]
    cosine, first, second = cos_ref[...], first_ref[...], second_ref[...]
    scale = 1.0 / math.sqrt(HD)
    width = grad_ref.shape[1] // 3

    def columns(which):
        return pl.ds(pl.multiple_of(which * width + pl.program_id(1) * LANES, LANES), LANES)

    def turned_back(field, start, end):
        ahead, behind = shifts(field)
        turned = field * cosine[start:end] - ahead * first[start:end] - behind * second[start:end]
        return turned.astype(BF)

    dk_sum[...] = jnp.zeros_like(dk_sum)
    dv_sum[...] = jnp.zeros_like(dv_sum)
    scaled, masks = lane_masks(scale), lane_masks(1.0)
    seg_col, seg_row = segc_ref[...], segr_ref[...]
    for block in range(q_ref.shape[0] // Q_BLOCK):
        start, end = block * Q_BLOCK, (block + 1) * Q_BLOCK
        keys, values = k_ref[:end, :], v_ref[:end, :]
        queries = by_head(q_ref[start:end, :], scaled)
        grads = by_head(g_ref[start:end, :], masks)
        probs = probs_of(queries, keys, allowed_of(seg_col, seg_row, block))
        grad_probs = mul_rows(values, grads)
        dots = jnp.sum(probs * grad_probs, axis=0, keepdims=True)
        grad_scores = (probs * (grad_probs - dots)).astype(BF)
        dv_sum[:end, :] += jnp.dot(probs.astype(BF), grads, preferred_element_type=F32)
        dk_sum[:end, :] += jnp.dot(grad_scores, queries, preferred_element_type=F32)
        dq_rows = joined(weight_grad(grad_scores, keys), masks) * scale
        grad_ref[start:end, columns(0)] = turned_back(dq_rows, start, end)
    grad_ref[:, columns(1)] = turned_back(dk_sum[...], 0, dk_sum.shape[0])
    grad_ref[:, columns(2)] = dv_sum[...].astype(BF)


def of_sequence(shape):
    return pl.BlockSpec(shape, lambda step, seq: (seq, 0))


def row_of_sequence(count_tok):
    return pl.BlockSpec((None, 1, count_tok), lambda step, seq: (seq, 0, 0))


def attend(normed_in, weight, bias_row, tables, seg_col, seg_row):
    count_tok = seg_row.shape[2]
    rows, cols = normed_in.shape[0], weight.shape[0] // 3
    steps = cols // LANES
    head_cols = pl.BlockSpec((count_tok, LANES), lambda step, seq: (seq, step))

    def part(which):
        return pl.BlockSpec((LANES, D), lambda step, seq: (which * steps + step, 0))

    def bias_part(which):
        return pl.BlockSpec((1, LANES), lambda step, seq: (0, which * steps + step))

    return pl.pallas_call(
        attend_kernel,
        grid=(steps, rows // count_tok),
        in_specs=[of_sequence((count_tok, D))]
        + [part(i) for i in range(3)]
        + [bias_part(i) for i in range(3)]
        + [of_sequence((count_tok, LANES))] * 3
        + [of_sequence((count_tok, 1)), row_of_sequence(count_tok)],
        out_specs=[head_cols] * 4,
        out_shape=[jax.ShapeDtypeStruct((rows, cols), BF)] * 4,
        compiler_params=pltpu.CompilerParams(vmem_limit_bytes=48 << 20),
        cost_estimate=SHORT,
        name="attend",
    )(normed_in, weight, weight, weight, bias_row, bias_row, bias_row, *tables, seg_col, seg_row)


def attend_back(query, key_rot, value_in, grad_attended, tables, seg_col, seg_row, first_seq, others):
    count_tok = seg_row.shape[2]
    rows, cols = grad_attended.shape

    def of_heads(first):
        return pl.BlockSpec((count_tok, LANES), lambda seq, step: (seq + first, step))

    def of_seq(shape):
        return pl.BlockSpec(shape, lambda seq, step: (seq + first_seq, 0))

    operands = [query, key_rot, value_in, grad_attended, *tables, seg_col, seg_row]
    in_specs = (
        [of_heads(first_seq)] * 3
        + [of_heads(0)]
        + [of_seq((count_tok, LANES))] * 3
        + [of_seq((count_tok, 1))]
        + [pl.BlockSpec((None, 1, count_tok), lambda seq, step: (seq + first_seq, 0, 0))]
    )
    aliases = {}
    if others is not None:
        aliases = {len(operands): 0}
        operands.append(others)
        in_specs.append(pl.BlockSpec(memory_space=pl.ANY))
    return pl.pallas_call(
        attend_back_kernel,
        grid=(rows // count_tok, cols // LANES),
        in_specs=in_specs,
        out_specs=of_seq((count_tok, 3 * cols)),
        out_shape=jax.ShapeDtypeStruct((query.shape[0], 3 * cols), BF),
        scratch_shapes=[pltpu.VMEM((count_tok, LANES), F32)] * 2,
        input_output_aliases=aliases,
        compiler_params=pltpu.CompilerParams(vmem_limit_bytes=48 << 20),
        cost_estimate=SHORT,
        name="attend_back",
    )(*operands)


def rows_product(left, right, first_row, count_rows, right_rows=False):
    inner, cols = right.shape[::-1] if right_rows else right.shape
    width = 512

    def kernel(left_ref, right_ref, out_ref):
        if right_rows:
            out_ref[...] = mul_rows(left_ref[...], right_ref[...])
        else:
            out_ref[...] = jnp.dot(left_ref[...], right_ref[...], preferred_element_type=F32)

    if right_rows:
        right_spec = pl.BlockSpec((width, inner), lambda n: (n, 0))
    else:
        right_spec = pl.BlockSpec((inner, width), lambda n: (0, n))
    return pl.pallas_call(
        kernel,
        grid=(cols // width,),
        in_specs=[
            pl.BlockSpec((count_rows, inner), lambda n: (first_row // count_rows, 0)),
            right_spec,
        ],
        out_specs=pl.BlockSpec((count_rows, width), lambda n: (0, n)),
        out_shape=jax.ShapeDtypeStruct((count_rows, cols), F32),
        compiler_params=pltpu.CompilerParams(vmem_limit_bytes=48 << 20),
        cost_estimate=SHORT,
        name="rows_product",
    )(left, right)


def attention_grads(half, side_at, grad_proj, inputs, grad_attn, attended, line, group):
    count_rows, proj_cols = grad_proj.shape
    cols = attended.shape[1]
    qkv_rows, out_rows = proj_cols // (2 * line), D // (2 * line)
    share = out_rows // group
    width = D // 2
    members = width // cols
    rows = qkv_rows + share
    pair_rows = grad_attn[0].shape[0]

    def kernel(side_ref, proj_ref, input_ref, attended_ref, *refs):
        attn_refs, (away_ref, mine_ref) = refs[:-2], refs[-2:]
        qkv = weight_grad(proj_ref[...], input_ref[...])
        blocks = []
        for side in range(2):
            start = side * out_rows + half * (members * share)
            out = sum(
                weight_grad(
                    attn_ref[:, start : start + members * share],
                    attended_ref[pair * pair_rows : (pair + 1) * pair_rows, :],
                )
                for pair, attn_ref in enumerate(attn_refs)
            )
            out = jnp.concatenate([out[m * share : (m + 1) * share] for m in range(members)], axis=1)
            blocks.append((qkv[side * qkv_rows : (side + 1) * qkv_rows], out))

        def store(mine, away):
            mine_ref[:qkv_rows, :] = blocks[mine][0]
            mine_ref[qkv_rows:, :] = blocks[mine][1]
            away_ref[:qkv_rows, :] = blocks[away][0].astype(BF)
            away_ref[qkv_rows:, :] = blocks[away][1].astype(BF)

        pl.when(side_ref[0] == 0)(lambda: store(0, 1))
        pl.when(side_ref[0] != 0)(lambda: store(1, 0))

    out_block = pl.BlockSpec((None, rows, width), lambda z, side: (z, 0, 0))
    return pl.pallas_call(
        kernel,
        grid_spec=pltpu.PrefetchScalarGridSpec(
            num_scalar_prefetch=1,
            grid=(line,),
            in_specs=[
                pl.BlockSpec((count_rows, 2 * qkv_rows), lambda z, side: (0, z)),
                pl.BlockSpec((count_rows, width), lambda z, side: (0, half)),
                pl.BlockSpec((count_rows, cols), lambda z, side: (0, 0)),
            ]
            + [pl.BlockSpec((pair_rows, 2 * out_rows), lambda z, side: (0, z))] * len(grad_attn),
            out_specs=[out_block, out_block],
        ),
        out_shape=[
            jax.ShapeDtypeStruct((line, rows, width), BF),
            jax.ShapeDtypeStruct((line, rows, width), F32),
        ],
        compiler_params=pltpu.CompilerParams(vmem_limit_bytes=56 << 20),
        cost_estimate=SHORT,
        name="attention_grads",
    )(side_at.reshape(1), grad_proj, inputs, attended, *grad_attn)


class Layout:
    def __init__(self, n_wide, n_narrow):
        self.narrow = n_narrow
        self.count = n_wide * n_narrow
        self.group = 2 * n_narrow
        self.outer = n_wide // 2
        self.line = self.outer // 2
        self.core_mask = n_narrow
        self.side_mask = 2 * n_narrow
        self.line_mask = 4 * n_narrow
        self.shifts = list(range(1, n_narrow))
        self.outer_groups = [
            [o * self.group + member for o in range(self.outer)] for member in range(self.group)
        ]

    def swap(self, value, mask):
        return lax.ppermute(value, AXES, [(i, i ^ mask) for i in range(self.count)])


    def gather_pairs(self, value, meanwhile=None):
        own = (value, self.swap(value, self.core_mask))
        shifted = [self.swap(value, mask) for mask in self.shifts]
        done = None
        if meanwhile is not None:
            shifted, done = lax.optimization_barrier((shifted, meanwhile(own)))
        return [own] + [(block, self.swap(block, self.core_mask)) for block in shifted], done

    def across_cores(self, partials):
        summed = []
        for partial in partials:
            own, sent = jnp.split(partial, 2)
            summed.append(own + self.swap(sent.astype(BF), self.core_mask).astype(F32))
        return summed

    def across_shifts(self, summed, meanwhile=None):
        shifted = [self.swap(part.astype(BF), mask) for part, mask in zip(summed[1:], self.shifts)]
        if meanwhile is not None:
            shifted, meanwhile = lax.optimization_barrier((shifted, meanwhile))
        return sum((part.astype(F32) for part in shifted), start=summed[0]), meanwhile

    def swap_group(self, pieces, member):
        result = jnp.zeros(pieces.shape, pieces.dtype)
        for mask in range(self.group):
            piece = lax.dynamic_index_in_dim(pieces, member ^ mask, 0, keepdims=False)
            if mask:
                piece = self.swap(piece, mask)
            result = lax.dynamic_update_index_in_dim(result, piece, member ^ mask, 0)
        return result


    def gather_outer(self, value):
        return lax.all_gather(value, AXES, axis=0, axis_index_groups=self.outer_groups)

    def scatter_outer(self, value):
        return lax.psum_scatter(
            value, AXES, scatter_dimension=0, tiled=True, axis_index_groups=self.outer_groups
        )

    def by_side(self, grad, place):
        by_place = grad.reshape(self.line, 2, -1, grad.shape[1])
        away = lax.dynamic_index_in_dim(by_place, 1 - place % 2, 1, keepdims=False).astype(BF)
        return away, lax.dynamic_index_in_dim(by_place, place % 2, 1, keepdims=False)

    def across_sides(self, away, mine):
        return mine + self.swap(away, self.side_mask).astype(F32)

    def line_steps(self):
        return [1 << bit for bit in range(self.line.bit_length() - 1)]

    def along_line(self, mine, place, step):
        pairs = mine.reshape(-1, 2, *mine.shape[1:])
        at = place // 2 // step % 2
        away = lax.dynamic_index_in_dim(pairs, 1 - at, 1, keepdims=False).astype(BF)
        mine = lax.dynamic_index_in_dim(pairs, at, 1, keepdims=False)
        return mine + self.swap(away, step * self.line_mask).astype(F32)


    def gather_small(self, row, index):
        blocks = row
        mask = 1
        while mask < self.line_mask:
            blocks = jnp.concatenate([blocks, self.swap(blocks, mask)])
            mask *= 2
        blocks = jnp.concatenate(
            [blocks] + [self.swap(blocks, step * self.line_mask) for step in range(1, self.line)]
        )
        return jnp.dot(self.by_mask(index).astype(row.dtype), blocks, preferred_element_type=F32)

    def scatter_small_line(self, rows, index):
        rows = jnp.dot(self.by_mask(index).astype(F32), rows, precision=lax.Precision.HIGHEST)
        blocks = jnp.split(rows, self.line)
        total = blocks[0]
        for step in range(1, self.line):
            total = total + self.swap(blocks[step], step * self.line_mask)
        return total

    def scatter_small_rest(self, total):
        mask = self.side_mask
        while mask:
            total = total[:mask] + self.swap(total[mask:], mask)
            mask //= 2
        return total

    def by_mask(self, index):
        numbers = jnp.arange(self.count, dtype=jnp.int32)
        return (numbers[:, None] ^ numbers[None, :]) == index


def deal_heads(layout, weight, member):
    per, group = weight.shape[0] // HD, layout.group
    got = [
        lax.ppermute(
            block,
            AXES,
            [(i, i // group * group + (per * i + j) % group) for i in range(layout.count)],
        )
        for j, block in enumerate(jnp.split(weight, per))
    ]
    stacked = jnp.stack(got)
    order = [lax.rem(k * group + member, per) for k in range(per)]
    return jnp.concatenate(
        [lax.dynamic_index_in_dim(stacked, j, 0, keepdims=False) for j in order]
    )


def deal_back(layout, rows, member):
    per, group = rows.shape[0] // HD, layout.group
    blocks = rows.reshape(per, HD, rows.shape[1])
    result = []
    for j in range(per):
        chosen = blocks[0]
        for k in range(1, per):
            chosen = jnp.where(lax.rem(k * group + member, per) == j, blocks[k], chosen)
        pairs = [(i // group * group + (per * i + j) % group, i) for i in range(layout.count)]
        result.append(lax.ppermute(chosen, AXES, pairs))
    return jnp.concatenate(result)


def heads_dealt(layout, qkv_rows):
    return qkv_rows % HD == 0 and math.gcd(qkv_rows // HD, layout.group) == 1


def gather_attention(layout, qkv_weight, out_weight, member):
    qkv_rows, share = qkv_weight.shape[0], out_weight.shape[0]
    cols = D // layout.group
    out_pieces = jnp.transpose(
        out_weight.reshape(share, H // layout.group, layout.group, HD), (2, 0, 1, 3)
    ).reshape(layout.group, share, cols)
    out_mine = layout.swap_group(out_pieces, member)
    out_mine = out_mine.reshape(layout.group * share, cols)
    if not heads_dealt(layout, qkv_rows):
        full = lax.all_gather(qkv_weight, AXES, axis=0, tiled=True)
        split = full.reshape(3 * H // layout.group, layout.group, HD, D)
        mine = lax.dynamic_index_in_dim(split, member, 1, keepdims=False).reshape(-1, D)
        return mine, layout.gather_outer(out_mine).reshape(D, cols)
    both = jnp.concatenate([deal_heads(layout, qkv_weight, member), out_mine.reshape(share, D)])
    full = layout.gather_outer(both)
    return full[:, :qkv_rows].reshape(-1, D), full[:, qkv_rows:].reshape(D, cols)


def scatter_attention(layout, grad_proj, inputs, grad_attn, attended, qkv_rows, place, first, second):
    steps = layout.line_steps()
    if not heads_dealt(layout, qkv_rows):
        group = layout.group
        split = jnp.zeros((3 * H // group, group, HD, D), BF)
        grad = weight_grad(grad_proj, inputs).astype(BF).reshape(-1, 1, HD, D)
        split = lax.dynamic_update_index_in_dim(split, grad, lax.axis_index(AXES) % group, 1)
        qkv_sum = lax.psum_scatter(split.reshape(-1, D), AXES, scatter_dimension=0, tiled=True)
        out_own = weight_grad(jnp.concatenate(grad_attn), attended)
        out_sum = layout.across_sides(*layout.by_side(out_own, place))
        for step in steps:
            out_sum = layout.along_line(out_sum, place, step)
        return qkv_sum, out_sum[0].astype(BF), second(first(grad_proj))
    others = (inputs, grad_attn, attended, layout.line, layout.group)
    away, mine = attention_grads(0, place % 2, grad_proj, *others)
    away, mine, grad_proj = lax.optimization_barrier((away, mine, grad_proj))
    left = layout.across_sides(away, mine)
    away, mine = attention_grads(1, place % 2, grad_proj, *others)
    left, away, mine, done = lax.optimization_barrier((left, away, mine, first(grad_proj)))
    left = layout.along_line(left, place, steps[0])
    right = layout.across_sides(away, mine)
    left, right, done = lax.optimization_barrier((left, right, second(done)))
    for step in steps[1:]:
        left = layout.along_line(left, place, step)
    right = layout.along_line(right, place, steps[0])
    left, right, last = lax.optimization_barrier((left, right, done[0]))
    done = (last, *done[1:])
    for step in steps[1:]:
        right = layout.along_line(right, place, step)
    summed = jnp.concatenate([left[0].astype(BF), right[0].astype(BF)], axis=1)
    out_sum = summed[qkv_rows:].reshape(-1, layout.group, D // layout.group)
    return summed[:qkv_rows], jnp.transpose(out_sum, (1, 0, 2)).reshape(-1, D // layout.group), done


def per_device(
    layout,
    tokens,
    segment_ids,
    language_ids,
    lang_table,
    norm1_gain,
    norm1_bias,
    qkv_weight,
    qkv_bias,
    out_weight,
    norm2_gain,
    norm2_bias,
    gate_up_weight,
    down_weight,
    cotangent,
):
    count_tok = tokens.shape[0]
    group, outer, count, narrow = layout.group, layout.outer, layout.count, layout.narrow
    index = lax.axis_index(AXES)
    member, place = lax.rem(index, group), index // group
    share = D // count
    unit_rows = gate_up_weight.shape[0]
    units = FF // group
    head_cols = D // group

    small = jnp.concatenate(
        [
            lang_table.T,
            norm1_gain[None],
            norm1_bias[None],
            norm2_gain[None],
            norm2_bias[None],
            qkv_bias.reshape(3, share),
        ]
    )
    small_len = SMALL_ROWS * share
    small_all = layout.gather_small(small.reshape(1, small_len), index)
    small_all = small_all.reshape(count, SMALL_ROWS, share)
    small_rows = jnp.transpose(small_all, (1, 0, 2)).reshape(SMALL_ROWS, D)
    table_rows = small_rows[:LANGS].astype(BF)
    gain1, bias1, gain2, bias2 = (small_rows[LANGS + i] for i in range(4))
    bias_heads = small_all[:, LANGS + 4 :].reshape(3, H // group, group, HD)
    bias_row = lax.dynamic_index_in_dim(bias_heads, member, 2, keepdims=False).reshape(
        1, 3 * head_cols
    )

    qkv_part, out_part = gather_attention(layout, qkv_weight, out_weight, member)
    gate_up_part = layout.gather_outer(gate_up_weight).reshape(2 * units, D)
    down_pieces = jnp.transpose(
        down_weight.reshape(share, outer // 2, group, unit_rows), (2, 0, 1, 3)
    ).reshape(group, share, units)
    down_mine = layout.swap_group(down_pieces, member).reshape(group * share, units)

    segment_pairs, _ = layout.gather_pairs(segment_ids)
    segment_rows = [row for pair in segment_pairs for row in pair]
    seg_row = jnp.stack(segment_rows)
    seg_col = seg_row.reshape(group * count_tok, 1)
    tables = tuple(
        jnp.concatenate(parts) for parts in zip(*(rotary_tables(row[0]) for row in segment_rows))
    )
    one_hot = language_ids[0][:, None] == jnp.arange(LANGS, dtype=jnp.int32)[None, :]
    stream0 = tokens.astype(F32) + jnp.dot(
        one_hot.astype(BF), table_rows, preferred_element_type=F32
    )
    normed_in, norm1_hat, norm1_inv = layer_norm(stream0, gain1, bias1)
    in_pairs, _ = layout.gather_pairs(normed_in.astype(BF))
    in_group = jnp.concatenate(sum(in_pairs, ()))
    in_group, cotangent_late, down_mine = lax.optimization_barrier((in_group, cotangent, down_mine))
    down_part = layout.gather_outer(down_mine).reshape(D, units)
    cot_pairs, _ = layout.gather_pairs(cotangent_late)
    cot_group = jnp.concatenate(sum(cot_pairs, ()))
    query, key_rot, value_in, attended = attend(
        in_group, qkv_part, bias_row, tables, seg_col, seg_row
    )
    attended, cot_group = lax.optimization_barrier((attended, cot_group))
    pair_rows = 2 * count_tok

    def pair_of(value, pair):
        return value[pair * pair_rows : (pair + 1) * pair_rows]

    out_sums = layout.across_cores(
        [mul_rows(pair_of(attended, pair), out_part) for pair in range(narrow)]
    )
    stream1 = stream0 + layout.across_shifts(out_sums)[0]

    normed_mid, norm2_hat, norm2_inv = layer_norm(stream1, gain2, bias2)
    mid_pairs, _ = layout.gather_pairs(normed_mid.astype(BF))
    mid_group = jnp.concatenate(sum(mid_pairs, ()))
    gate_up = mul_rows(mid_group, gate_up_part)
    gate_part, up_part = gate_up[:, :units], gate_up[:, units:]
    sigma_gate = jax.nn.sigmoid(gate_part)
    silu_gate = gate_part * sigma_gate
    hidden = (silu_gate * up_part).astype(BF)
    down_own = weight_grad(cot_group, hidden).astype(BF)
    down_part, down_own = lax.optimization_barrier((down_part, down_own))
    down_sum = layout.scatter_outer(down_own)
    grad_hidden = jnp.dot(cot_group, down_part, preferred_element_type=F32)
    grad_gate = grad_hidden * up_part * (sigma_gate + gate_part * sigma_gate * (1.0 - sigma_gate))
    grad_gu = jnp.concatenate([grad_gate, grad_hidden * silu_gate], axis=1).astype(BF)
    mid_parts = {}
    for pair in reversed(range(narrow)):
        grad_rows = pair_of(grad_gu, pair)
        if pair + 1 in mid_parts:
            grad_rows, mid_parts[pair + 1] = lax.optimization_barrier((grad_rows, mid_parts[pair + 1]))
        mid_parts[pair] = jnp.dot(grad_rows, gate_up_part, preferred_element_type=F32)
    mid_sums = layout.across_cores([mid_parts[pair] for pair in range(narrow)])
    gate_up_own = weight_grad(grad_gu, mid_group).astype(BF)
    grad_mid, gate_up_own = layout.across_shifts(mid_sums, gate_up_own)
    gate_up_sum = layout.scatter_outer(gate_up_own)

    grad_norm2, gain2_grad, bias2_grad = norm_back(grad_mid, norm2_hat, norm2_inv, gain2)
    grad_stream1 = cotangent.astype(F32) + grad_norm2

    def back_of(pair, first_seq, others):
        grad_rows = jnp.concatenate(pair)
        grad_attended = jnp.dot(grad_rows, out_part, preferred_element_type=F32).astype(BF)
        grads = attend_back(
            query, key_rot, value_in, grad_attended, tables, seg_col, seg_row, first_seq, others
        )
        return grads, grad_rows

    def in_the_meantime(pair):
        return back_of(pair, 0, None)

    attn_pairs, (grad_proj, own_rows) = layout.gather_pairs(
        grad_stream1.astype(BF), in_the_meantime
    )
    grad_attn = [own_rows]
    for pair in range(1, narrow):
        grad_proj, grad_rows = back_of(attn_pairs[pair], 2 * pair, grad_proj)
        grad_attn.append(grad_rows)

    def input_grad(grad_proj):
        parts = [
            rows_product(grad_proj, qkv_part, pair * pair_rows, pair_rows) for pair in range(narrow)
        ]
        return layout.across_shifts(layout.across_cores(parts))[0], hidden

    def first_norm(grad_in):
        grad_norm1, gain1_grad, bias1_grad = norm_back(grad_in, norm1_hat, norm1_inv, gain1)
        grad_stream0 = grad_stream1 + grad_norm1
        lang_grad = lax.dot_general(
            one_hot.astype(F32),
            grad_stream0,
            (((0,), (0,)), ((), ())),
            precision=lax.Precision.HIGHEST,
        )
        bias_grad = jnp.zeros((3 * H // group, group, HD), F32)
        bias_grad = lax.dynamic_update_index_in_dim(
            bias_grad, jnp.sum(grad_proj.astype(F32), axis=0).reshape(-1, 1, HD), member, 1
        )
        rows = jnp.concatenate(
            [lang_grad, jnp.stack([gain1_grad, bias1_grad, gain2_grad, bias2_grad])]
        ).reshape(LANGS + 4, count, share)
        small_grad = jnp.concatenate(
            [jnp.transpose(rows, (1, 0, 2)), bias_grad.reshape(count, 3, share)], axis=1
        ).reshape(count, small_len)
        return grad_stream0.astype(BF), small_grad

    def meanwhile(done):
        grad_in, hidden = done
        token_grad, small_grad = first_norm(grad_in)
        small_line = layout.scatter_small_line(small_grad, index)
        mixed_parts = [
            rows_product(hidden, down_part, pair * pair_rows, pair_rows, right_rows=True)
            for pair in range(narrow)
        ]
        down_got = layout.swap_group(down_sum.reshape(group, share, units), member)
        return small_line, token_grad, mixed_parts, gate_up_sum, down_got

    qkv_sum, out_sum, (small_line, token_grad, mixed_parts, gate_up_sum, down_got) = scatter_attention(
        layout, grad_proj, in_group, grad_attn, attended, qkv_weight.shape[0], place, input_grad, meanwhile
    )
    mixed_sums = layout.across_cores(mixed_parts)
    small_sum = layout.scatter_small_rest(small_line).reshape(SMALL_ROWS, share)
    mixed = (stream1 + layout.across_shifts(mixed_sums)[0]).astype(BF)

    if heads_dealt(layout, qkv_weight.shape[0]):
        qkv_sum = deal_back(layout, qkv_sum, member)
    down_grad = jnp.transpose(
        down_got.reshape(group, share, outer // 2, unit_rows), (1, 2, 0, 3)
    ).reshape(share, FF)
    out_got = layout.swap_group(out_sum.reshape(group, share, head_cols), member)
    out_grad = jnp.transpose(
        out_got.reshape(group, share, H // group, HD), (1, 2, 0, 3)
    ).reshape(share, D)
    return (
        mixed,
        token_grad,
        small_sum[:LANGS].T,
        small_sum[LANGS],
        small_sum[LANGS + 1],
        qkv_sum.astype(F32),
        small_sum[LANGS + 4 :].reshape(3 * share),
        out_grad.astype(F32),
        small_sum[LANGS + 2],
        small_sum[LANGS + 3],
        gate_up_sum.astype(F32),
        down_grad.astype(F32),
    )


def solution(mesh):
    rows, vector = P(AXES, None), P(AXES)
    layout = Layout(mesh.shape["wide"], mesh.shape["narrow"])
    return jax.shard_map(
        functools.partial(per_device, layout),
        mesh=mesh,
        in_specs=(rows, rows, rows, rows, vector, vector, rows, vector, rows, vector, vector, rows, rows, rows),
        out_specs=(rows, rows, rows, vector, vector, rows, vector, rows, vector, vector, rows, rows),
        check_vma=False,
    )
```

time: 4640 us -> 887 us (0.19)
  waiting for transfers between devices: 4040 us -> 380 us
  matrix products: 297 us -> 125 us
  blocking collectives: 155 us -> 0 us
  Pallas kernels: 0 us -> 116 us
  starting transfers between devices: 0.82 us -> 65.5 us
  other arithmetic: 31.8 us -> 92 us
    reduce_scatter x3 -> x2, waiting for transfers between devices: 2650 us -> 5.38 us  [scatter_outer(): lax.psum_scatter(value, AXES, scatter_dimension=0, tiled=True, axis_index...]
    unnamed x11 -> x5, waiting for transfers between devices: 973 us -> 0.76 us
    all_gather x4 -> x3, waiting for transfers between devices: 410 us -> 53.4 us  [gather_outer(): lax.all_gather(value, AXES, axis=0, axis_index_groups=self.outer_groups)]
    ppermute x0 -> x63, waiting for transfers between devices: none -> 321 us  [the longest x57 314 us: swap(): return lax.ppermute(value, AXES, [(i, i ^ mask) for i in range(self.count)])]
    pallas_call x0 -> x9, Pallas kernels: none -> 116 us  [the longest x4 36.2 us: rows_product(): pl.pallas_call(kernel, grid=(cols // width,), in_specs=[pl.BlockSpec((cou...]
    unnamed x2 -> x0, blocking collectives: 105 us -> none
    dot_general x33 -> x9, matrix products: 132 us -> 52.1 us  [the longest x2 25.2 us: per_device(): jnp.dot(grad_rows, gate_up_part, preferred_element_type=F32)]
    ppermute x0 -> x63, starting transfers between devices: none -> 65.4 us  [the longest x57 53.3 us: swap(): return lax.ppermute(value, AXES, [(i, i ^ mask) for i in range(self.count)])]
  transfers between devices with their start and end apart: 9 -> 68, of which waited for: 8 -> 31; matrix products, arithmetic and copies ran while one was open for 6% -> 32% of each run, Pallas kernels for 0% -> 13%
where the time goes in v1:
time: 887 us; the launch traced here: 880 us
  waiting for transfers between devices  380 us (43%)
  matrix products  125 us (14%)
  Pallas kernels  116 us (13%)
  other arithmetic  92 us (10%)
  local copies, waits for them, and re-layouts  85 us (10%)
  starting transfers between devices  65.5 us (7%)
  between operations  15.7 us (2%)
    ppermute x57, waiting for transfers between devices, swap(): return lax.ppermute(value, AXES, [(i, i ^ mask) for i in range(self.count)])  314 us
    all_gather x3, waiting for transfers between devices, gather_outer(): lax.all_gather(value, AXES, axis=0, axis_index_groups=self.outer_groups)  53.4 us
    ppermute x57, starting transfers between devices, swap(): return lax.ppermute(value, AXES, [(i, i ^ mask) for i in range(self.count)])  53.3 us
    dot_general x2, matrix products, weight_grad(): lax.dot_general(grad_rows, inputs, (((0,), (0,)), ((), ())), preferred_el...  37.8 us
    pallas_call x4, Pallas kernels, rows_product(): pl.pallas_call(kernel, grid=(cols // width,), in_specs=[pl.BlockSpec((cou...  36.2 us
    dot_general x3, matrix products, mul_rows(): lax.dot_general(left, weight, (((1,), (1,)), ((), ())), preferred_element...  35.3 us
    pallas_call x1, Pallas kernels, attend(): pl.pallas_call(attend_kernel, grid=(steps, rows // count_tok), in_specs=[...  29.8 us
    pallas_call x2, Pallas kernels, attention_grads(): pl.pallas_call(kernel, grid_spec=pltpu.PrefetchScalarGridSpec(num_scalar_...  26.6 us
  transfers between devices with their start and end apart: 68, of which 31 were waited for; matrix products, arithmetic and copies ran while one was open for 32% of the time, Pallas kernels for 13%

profile of v1, /device:TPU:13, one launch (start us, length us, event | category | flops | bytes accessed | tf_op | source)
XLA Modules:
  0.0 879.8 jit_solution(9217148720045089038)
XLA Ops:
  15.3 6.9 collective-permute-done.13
  47.9 30.4 %collective-permute-done.7 = bf16[384,2048]{1,0:T(8,128)(2,1)} collective-permute-done((bf16[384,2048]{1,0:T(8,128)(2,1)}, bf16[384,2048]{1,0:T(8,128)(2,1)}, u32[]{:S(2)}, u32[]{:S(2)}) %collective-permute-start.7) | collective-permute-done | bytes 1572896 | tf_op jit(solution)/shard_map/ppermute | solution.py:344
  100.5 33.4 %collective-permute-done.19 = s32[1,384]{1,0:T(1,128)S(1)} collective-permute-done((s32[1,384]{1,0:T(1,128)S(1)}, s32[1,384]{1,0:T(1,128)S(1)}, u32[]{:S(2)}, u32[]{:S(2)}) %collective-permute-start.19) | collective-permute-done | bytes 1568 | tf_op jit(solution)/shard_map/ppermute | solution.py:344
  161.0 7.1 slice.151
  168.1 29.8 %attend.1 = (bf16[1536,512]{1,0:T(8,128)(2,1)S(1)}, bf16[1536,512]{1,0:T(8,128)(2,1)S(1)}, bf16[1536,512]{1,0:T(8,128)(2,1)S(1)}, bf16[1536,512]{1,0:T(8,128)(2,1)}) custom-call(bf16[1536,2048]{1,0:T(8,128)(2,1)} %pad_maximum_fusion.2.x_ref.input_ref, bf16[1536,2048]{1,0:T(8,128)(2,1)} %bitcast.156, bf16[1536,2048]{1,0:T(8,128)(2,1)} %bitcast.157, ...), custom_call_target="tpu_custom_call" | custom-call | flops 1 | bytes 1 | tf_op jit(solution)/shard_map/attend/pallas_call | solution.py:187
  220.4 35.0 %collective-permute-done.26 = bf16[384,2048]{1,0:T(8,128)(2,1)} collective-permute-done((bf16[384,2048]{1,0:T(8,128)(2,1)}, bf16[384,2048]{1,0:T(8,128)(2,1)}, u32[]{:S(2)}, u32[]{:S(2)}) %collective-permute-start.26) | collective-permute-done | bytes 1572896 | tf_op jit(solution)/shard_map/ppermute | solution.py:344
  263.8 33.4 %collective-permute-done.28 = bf16[384,2048]{1,0:T(8,128)(2,1)} collective-permute-done((bf16[384,2048]{1,0:T(8,128)(2,1)}, bf16[384,2048]{1,0:T(8,128)(2,1)}, u32[]{:S(2)}, u32[]{:S(2)}) %collective-permute-start.28) | collective-permute-done | bytes 1572896 | tf_op jit(solution)/shard_map/ppermute | solution.py:344
  299.3 13.5 %all-gather.11.cloned.1.call-done = bf16[2816,2048]{1,0:T(8,128)(2,1)} async-done(((bf16[352,2048]{1,0:T(8,128)(2,1)}), bf16[2816,2048]{1,0:T(8,128)(2,1)}) %all-gather.11.cloned.1.call-update) | async-done | bytes 11534352 | tf_op jit(solution)/shard_map/all_gather | solution.py:379
  312.8 29.7 %fusion.10 = f32[1536,2816]{1,0:T(8,128)} fusion(bf16[2816,2048]{1,0:T(8,128)(2,1)} %all-gather.11.cloned.1.call-done, bf16[384,2048]{1,0:T(8,128)(2,1)} %collective-permute-done.29, bf16[384,2048]{1,0:T(8,128)(2,1)} %collective-permute-done.28, bf16[384,2048]{1,0:T(8,128)(2,1)} %collective-permute-done.27, bf16[384,2048]{1,0:T(8,128)(2,1)} %add_convert_fusion.3), kind=kOutput, calls=%fused_computation.75 | convolution fusion | flops 17741905920 | bytes 35127296 | tf_op jit(solution)/shard_map/dot_general | solution.py:66
  342.5 7.2 multiply_convert_fusion.2.left_ref
  349.8 13.9 %convolution_convert_fusion.1 = bf16[2048,1408]{1,0:T(8,128)(2,1)} fusion(bf16[1536,2048]{1,0:T(8,128)(2,1)} %pad_maximum_fusion.3, bf16[1536,1408]{1,0:T(8,128)(2,1)S(1)} %multiply_convert_fusion.2.left_ref), kind=kOutput, calls=%fused_computation.12 | convolution fusion | flops 8861253632 | bytes 16384000 | tf_op jit(solution)/shard_map/dot_general | solution.py:70
  365.8 40.0 %all-gather.9.cloned.1.call-done.right_ref = bf16[2048,1408]{1,0:T(8,128)(2,1)} async-done(((bf16[256,1408]{1,0:T(8,128)(2,1)}), bf16[2048,1408]{1,0:T(8,128)(2,1)}) %all-gather.9.cloned.1.call-update) | async-done | bytes 5767184 | tf_op jit(solution)/shard_map/all_gather | solution.py:379
  405.9 21.1 %multiply_convert_fusion = (bf16[1536,1408]{1,0:T(8,128)(2,1)S(1)}, bf16[1536,1408]{1,0:T(8,128)(2,1)}) fusion(f32[1536,2816]{1,0:T(8,128)} %fusion.10, bf16[1536,2048]{1,0:T(8,128)(2,1)} %pad_maximum_fusion.3, bf16[2048,1408]{1,0:T(8,128)(2,1)} %all-gather.9.cloned.1.call-done.right_ref), kind=kOutput, calls=%fused_computation.7 | convolution fusion | flops 8884322304 | bytes 38010880 | tf_op jit(solution)/shard_map/dot_general | solution.py:619
  431.1 12.0 %fusion.2 = f32[768,2048]{1,0:T(8,128)S(1)} fusion(bf16[2816,2048]{1,0:T(8,128)(2,1)} %all-gather.11.cloned.1.call-done, bf16[1536,1408]{1,0:T(8,128)(2,1)S(1)} %copy-done.23, bf16[1536,1408]{1,0:T(8,128)(2,1)S(1)} %get-tuple-element.113), kind=kOutput, calls=%fused_computation.18 | convolution fusion | flops 8867020800 | bytes 26476544 | tf_op jit(solution)/shard_map/dot_general | solution.py:627
  450.1 23.9 %convolution_convert_fusion = bf16[2816,2048]{1,0:T(8,128)(2,1)} fusion(bf16[1536,1408]{1,0:T(8,128)(2,1)S(1)} %get-tuple-element.113, bf16[1536,1408]{1,0:T(8,128)(2,1)} %get-tuple-element.114, bf16[384,2048]{1,0:T(8,128)(2,1)} %collective-permute-done.29, bf16[384,2048]{1,0:T(8,128)(2,1)} %collective-permute-done.28, ...), kind=kOutput, calls=%fused_computation | convolution fusion | flops 17764974592 | bytes 26476544 | tf_op jit(solution)/shard_map/dot_general | solution.py:70
  474.0 11.8 %collective-permute-done.32 = bf16[384,2048]{1,0:T(8,128)(2,1)} collective-permute-done((bf16[384,2048]{1,0:T(8,128)(2,1)}, bf16[384,2048]{1,0:T(8,128)(2,1)}, u32[]{:S(2)}, u32[]{:S(2)}) %collective-permute-start.32) | collective-permute-done | bytes 1572896 | tf_op jit(solution)/shard_map/ppermute | solution.py:344
  485.8 13.2 %fusion.53 = f32[768,2048]{1,0:T(8,128)S(1)} fusion(bf16[768,2816]{1,0:T(8,128)(2,1)} %fusion, bf16[2816,2048]{1,0:T(8,128)(2,1)} %all-gather.11.cloned.1.call-done), kind=kOutput, calls=%fused_computation.225 | convolution fusion | flops 8858370048 | bytes 22151168 | tf_op jit(solution)/shard_map/dot_general | solution.py:627
  515.0 11.7 %attend_back.2.rest_0_ = bf16[1536,1536]{1,0:T(8,128)(2,1)} custom-call(bf16[1536,512]{1,0:T(8,128)(2,1)S(1)} %get-tuple-element.57.q_ref, bf16[1536,512]{1,0:T(8,128)(2,1)S(1)} %copy-done.3, bf16[1536,512]{1,0:T(8,128)(2,1)} %copy-done.5, bf16[768,512]{1,0:T(8,128)(2,1)S(1)} %convolution_convert_fusion.3.g_ref, f32[1536,256]{1,0:T(8,128)} %pad_maximum_fusion.6.cos_ref, ...), custom_call_target="tpu_custom_call" | custom-call | flops 1 | bytes 1 | tf_op jit(solution)/shard_map/attend_back/pallas_call | solution.py:226
  528.8 17.3 %collective-permute-done.33 = bf16[384,2048]{1,0:T(8,128)(2,1)} collective-permute-done((bf16[384,2048]{1,0:T(8,128)(2,1)S(1)}, bf16[384,2048]{1,0:T(8,128)(2,1)}, u32[]{:S(2)}, u32[]{:S(2)}) %collective-permute-start.33) | collective-permute-done | bytes 1572896 | tf_op jit(solution)/shard_map/ppermute | solution.py:344
  554.6 11.6 %attend_back.3.proj_ref.left_ref = bf16[1536,1536]{1,0:T(8,128)(2,1)} custom-call(bf16[1536,512]{1,0:T(8,128)(2,1)S(1)} %get-tuple-element.57.q_ref, bf16[1536,512]{1,0:T(8,128)(2,1)S(1)} %copy-done.4, bf16[1536,512]{1,0:T(8,128)(2,1)} %copy-done.5, bf16[768,512]{1,0:T(8,128)(2,1)S(1)} %convolution_convert_fusion.2.g_ref, ...), custom_call_target="tpu_custom_call", output_to_operand_aliasing={{}: (9, {})} | custom-call | flops 1 | bytes 1 | tf_op jit(solution)/shard_map/attend_back/pallas_call | solution.py:226
  566.2 13.2 %attention_grads.2 = (bf16[4,256,1024]{2,1,0:T(8,128)(2,1)}, f32[4,256,1024]{2,1,0:T(8,128)}) custom-call(s32[1]{0:T(128)} %bitcast.46.side_ref, bf16[1536,1536]{1,0:T(8,128)(2,1)} %attend_back.3.proj_ref.left_ref, bf16[1536,2048]{1,0:T(8,128)(2,1)} %pad_maximum_fusion.2.x_ref.input_ref, bf16[1536,512]{1,0:T(8,128)(2,1)} %get-tuple-element.56.attended_ref, ...), custom_call_target="tpu_custom_call" | custom-call | flops 1 | bytes 1 | tf_op jit(solution)/shard_map/attention_grads/pallas_call | solution.py:305
  579.5 9.1 %rows_product.5 = f32[768,2048]{1,0:T(8,128)} custom-call(bf16[1536,1536]{1,0:T(8,128)(2,1)S(1)} %bitcast.152, bf16[1536,2048]{1,0:T(8,128)(2,1)} %bitcast.159), custom_call_target="tpu_custom_call" | custom-call | flops 1 | bytes 1 | tf_op jit(solution)/shard_map/rows_product/pallas_call | solution.py:254
  591.4 9.0 %rows_product.4 = f32[768,2048]{1,0:T(8,128)} custom-call(bf16[1536,1536]{1,0:T(8,128)(2,1)S(1)} %bitcast.152, bf16[1536,2048]{1,0:T(8,128)(2,1)} %bitcast.160), custom_call_target="tpu_custom_call" | custom-call | flops 1 | bytes 1 | tf_op jit(solution)/shard_map/rows_product/pallas_call | solution.py:254
  606.2 13.4 %attention_grads.3 = (bf16[4,256,1024]{2,1,0:T(8,128)(2,1)}, f32[4,256,1024]{2,1,0:T(8,128)}) custom-call(s32[1]{0:T(128)} %bitcast.46.side_ref, bf16[1536,1536]{1,0:T(8,128)(2,1)} %attend_back.3.proj_ref.left_ref, bf16[1536,2048]{1,0:T(8,128)(2,1)} %pad_maximum_fusion.2.x_ref.input_ref, bf16[1536,512]{1,0:T(8,128)(2,1)} %get-tuple-element.56.attended_ref, ...), custom_call_target="tpu_custom_call" | custom-call | flops 1 | bytes 1 | tf_op jit(solution)/shard_map/attention_grads/pallas_call | solution.py:305
  620.6 34.4 %collective-permute-done.36 = bf16[4,256,1024]{2,1,0:T(8,128)(2,1)} collective-permute-done((bf16[4,256,1024]{2,1,0:T(8,128)(2,1)}, bf16[4,256,1024]{2,1,0:T(8,128)(2,1)}, u32[]{:S(2)}, u32[]{:S(2)}) %collective-permute-start.36) | collective-permute-done | bytes 2097184 | tf_op jit(solution)/shard_map/ppermute | solution.py:344
  674.2 9.1 %rows_product.7 = f32[768,2048]{1,0:T(8,128)} custom-call(bf16[1536,1408]{1,0:T(8,128)(2,1)S(1)} %copy-done.1, bf16[2048,1408]{1,0:T(8,128)(2,1)} %all-gather.9.cloned.1.call-done.right_ref), custom_call_target="tpu_custom_call" | custom-call | flops 1 | bytes 1 | tf_op jit(solution)/shard_map/rows_product/pallas_call | solution.py:254
  683.2 9.0 %rows_product.6 = f32[768,2048]{1,0:T(8,128)} custom-call(bf16[1536,1408]{1,0:T(8,128)(2,1)S(1)} %copy-done.1, bf16[2048,1408]{1,0:T(8,128)(2,1)} %all-gather.9.cloned.1.call-done.right_ref), custom_call_target="tpu_custom_call" | custom-call | flops 1 | bytes 1 | tf_op jit(solution)/shard_map/rows_product/pallas_call | solution.py:254
  694.4 7.5 collective-permute-start.46
  702.8 26.8 %collective-permute-done.41 = bf16[4,256,1024]{2,1,0:T(8,128)(2,1)} collective-permute-done((bf16[4,256,1024]{2,1,0:T(8,128)(2,1)}, bf16[4,256,1024]{2,1,0:T(8,128)(2,1)}, u32[]{:S(2)}, u32[]{:S(2)}) %collective-permute-start.41) | collective-permute-done | bytes 2097184 | tf_op jit(solution)/shard_map/ppermute | solution.py:344
  752.0 28.7 %collective-permute-done.51 = bf16[1,256,1024]{2,1,0:T(8,128)(2,1)} collective-permute-done((bf16[1,256,1024]{2,1,0:T(8,128)(2,1)S(1)}, bf16[1,256,1024]{2,1,0:T(8,128)(2,1)}, u32[]{:S(2)}, u32[]{:S(2)}) %collective-permute-start.51) | collective-permute-done | bytes 524320 | tf_op jit(solution)/shard_map/ppermute | solution.py:344
  813.8 13.9 %collective-permute-done.56 = bf16[1,256,1024]{2,1,0:T(8,128)(2,1)} collective-permute-done((bf16[1,256,1024]{2,1,0:T(8,128)(2,1)S(1)}, bf16[1,256,1024]{2,1,0:T(8,128)(2,1)}, u32[]{:S(2)}, u32[]{:S(2)}) %collective-permute-start.56) | collective-permute-done | bytes 524320 | tf_op jit(solution)/shard_map/ppermute | solution.py:344
  833.9 15.7 %collective-permute-done.60 = bf16[64,512]{1,0:T(8,128)(2,1)S(1)} collective-permute-done((bf16[64,512]{1,0:T(8,128)(2,1)S(1)}, bf16[64,512]{1,0:T(8,128)(2,1)S(1)}, u32[]{:S(2)}, u32[]{:S(2)}) %collective-permute-start.60) | collective-permute-done | bytes 65568 | tf_op jit(solution)/shard_map/ppermute | solution.py:344
  (465 shorter events, 271.4 us)
Async XLA Ops:
  7.2 153.8 %all-gather.7.cloned.1.call-start = ((), (), s32[]{:S(2)}) async-start(), calls=%async_computation.4 | async-start | bytes 9437184 | tf_op jit(solution)/shard_map/all_gather | solution.py:379
  23.5 289.3 %all-gather.11.cloned.1.call-start = ((), (), s32[]{:S(2)}) async-start(), calls=%async_computation.6 | async-start | bytes 12976128 | tf_op jit(solution)/shard_map/all_gather | solution.py:379
  24.2 381.6 %all-gather.9.cloned.1.call-start = ((), (), s32[]{:S(2)}) async-start(), calls=%async_computation.5 | async-start | bytes 6488064 | tf_op jit(solution)/shard_map/all_gather | solution.py:379
  43.7 34.5 %collective-permute-start.7 = (bf16[384,2048]{1,0:T(8,128)(2,1)}, bf16[384,2048]{1,0:T(8,128)(2,1)}, u32[]{:S(2)}, u32[]{:S(2)}) collective-permute-start(bf16[384,2048]{1,0:T(8,128)(2,1)} %add_convert_fusion.4), channel_id=1, source_target_pairs={{0,1},{1,0},{2,3},{3,2},{4,5},{5,4},{6,7},{7,6},{8,9},{9,8},{10,11... | collective-permute-start | bytes 4718600 | tf_op jit(solution)/shard_map/ppermute | solution.py:344
  45.8 45.8 %collective-permute-start.6 = (bf16[384,2048]{1,0:T(8,128)(2,1)}, bf16[384,2048]{1,0:T(8,128)(2,1)S(1)}, u32[]{:S(2)}, u32[]{:S(2)}) collective-permute-start(bf16[384,2048]{1,0:T(8,128)(2,1)} %add_convert_fusion.4), channel_id=1, source_target_pairs={{0,2},{1,3},{2,0},{3,1},{4,6},{5,7},{6,4},{7,5},{8,10},{9,11},{10,... | collective-permute-start | bytes 4718600 | tf_op jit(solution)/shard_map/ppermute | solution.py:344
  97.6 38.5 %collective-permute-start.22 = (bf16[384,2048]{1,0:T(8,128)(2,1)S(1)}, bf16[384,2048]{1,0:T(8,128)(2,1)}, u32[]{:S(2)}, u32[]{:S(2)}) collective-permute-start(bf16[384,2048]{1,0:T(8,128)(2,1)S(1)} %copy-done.21), channel_id=1, source_target_pairs={{0,1},{1,0},{2,3},{3,2},{4,5},{5,4},{6,7},{7,6},{8,9},{9,8},{10,11... | collective-permute-start | bytes 4718600 | tf_op jit(solution)/shard_map/ppermute | solution.py:344
  97.7 36.3 %collective-permute-start.19 = (s32[1,384]{1,0:T(1,128)S(1)}, s32[1,384]{1,0:T(1,128)S(1)}, u32[]{:S(2)}, u32[]{:S(2)}) collective-permute-start(s32[1,384]{1,0:T(1,128)S(1)} %copy-done.53), channel_id=1, source_target_pairs={{0,1},{1,0},{2,3},{3,2},{4,5},{5,4},{6,7},{7,6},{8,9},{9,8},{10,11... | collective-permute-start | bytes 4616 | tf_op jit(solution)/shard_map/ppermute | solution.py:344
  99.1 35.5 %collective-permute-start.18 = (s32[1,384]{1,0:T(1,128)S(1)}, s32[1,384]{1,0:T(1,128)S(1)}, u32[]{:S(2)}, u32[]{:S(2)}) collective-permute-start(s32[1,384]{1,0:T(1,128)S(1)} %copy-done.53), channel_id=1, source_target_pairs={{0,2},{1,3},{2,0},{3,1},{4,6},{5,7},{6,4},{7,5},{8,10},{9,11},{10,... | collective-permute-start | bytes 4616 | tf_op jit(solution)/shard_map/ppermute | solution.py:344
  219.5 35.9 %collective-permute-start.26 = (bf16[384,2048]{1,0:T(8,128)(2,1)}, bf16[384,2048]{1,0:T(8,128)(2,1)}, u32[]{:S(2)}, u32[]{:S(2)}) collective-permute-start(bf16[384,2048]{1,0:T(8,128)(2,1)} %fusion.7), channel_id=1, source_target_pairs={{0,1},{1,0},{2,3},{3,2},{4,5},{5,4},{6,7},{7,6},{8,9},{9,8},{10,11... | collective-permute-start | bytes 4718600 | tf_op jit(solution)/shard_map/ppermute | solution.py:344
  262.1 35.1 %collective-permute-start.28 = (bf16[384,2048]{1,0:T(8,128)(2,1)}, bf16[384,2048]{1,0:T(8,128)(2,1)}, u32[]{:S(2)}, u32[]{:S(2)}) collective-permute-start(bf16[384,2048]{1,0:T(8,128)(2,1)} %add_convert_fusion.3), channel_id=1, source_target_pairs={{0,1},{1,0},{2,3},{3,2},{4,5},{5,4},{6,7},{7,6},{8,9},{9,8},{10,11... | collective-permute-start | bytes 4718600 | tf_op jit(solution)/shard_map/ppermute | solution.py:344
  262.2 430.4 %reduce-scatter.5.cloned.1.call-start = ((), (), s32[]{:S(2)}) async-start(), calls=%async_computation.3 | async-start | bytes 6488064 | tf_op jit(solution)/shard_map/reduce_scatter | solution.py:382
  262.3 37.0 %collective-permute-start.27 = (bf16[384,2048]{1,0:T(8,128)(2,1)}, bf16[384,2048]{1,0:T(8,128)(2,1)}, u32[]{:S(2)}, u32[]{:S(2)}) collective-permute-start(bf16[384,2048]{1,0:T(8,128)(2,1)} %add_convert_fusion.3), channel_id=1, source_target_pairs={{0,2},{1,3},{2,0},{3,1},{4,6},{5,7},{6,4},{7,5},{8,10},{9,11},{10,... | collective-permute-start | bytes 4718600 | tf_op jit(solution)/shard_map/ppermute | solution.py:344
  405.8 335.1 %reduce-scatter.3.cloned.1.call-start = ((), (), s32[]{:S(2)}) async-start(), calls=%async_computation.2 | async-start | bytes 12976128 | tf_op jit(solution)/shard_map/reduce_scatter | solution.py:382
  449.8 35.9 %collective-permute-start.32 = (bf16[384,2048]{1,0:T(8,128)(2,1)}, bf16[384,2048]{1,0:T(8,128)(2,1)}, u32[]{:S(2)}, u32[]{:S(2)}) collective-permute-start(bf16[384,2048]{1,0:T(8,128)(2,1)} %add_convert_fusion.2), channel_id=1, source_target_pairs={{0,1},{1,0},{2,3},{3,2},{4,5},{5,4},{6,7},{7,6},{8,9},{9,8},{10,11... | collective-permute-start | bytes 4718600 | tf_op jit(solution)/shard_map/ppermute | solution.py:344
  510.2 35.9 %collective-permute-start.33 = (bf16[384,2048]{1,0:T(8,128)(2,1)S(1)}, bf16[384,2048]{1,0:T(8,128)(2,1)}, u32[]{:S(2)}, u32[]{:S(2)}) collective-permute-start(bf16[384,2048]{1,0:T(8,128)(2,1)S(1)} %get-tuple-element.108), channel_id=1, source_target_pairs={{0,1},{1,0},{2,3},{3,2},{4,5},{5,4},{6,7},{7,6},{8,9},{9,8},{10,11... | collective-permute-start | bytes 4718600 | tf_op jit(solution)/shard_map/ppermute | solution.py:344
  591.2 63.8 %collective-permute-start.36 = (bf16[4,256,1024]{2,1,0:T(8,128)(2,1)}, bf16[4,256,1024]{2,1,0:T(8,128)(2,1)}, u32[]{:S(2)}, u32[]{:S(2)}) collective-permute-start(bf16[4,256,1024]{2,1,0:T(8,128)(2,1)} %get-tuple-element.72), channel_id=1, source_target_pairs={{0,4},{1,5},{2,6},{3,7},{4,0},{5,1},{6,2},{7,3},{8,12},{9,13},{10,... | collective-permute-start | bytes 6291464 | tf_op jit(solution)/shard_map/ppermute | solution.py:344
  603.6 55.0 %collective-permute-start.37 = (bf16[384,2048]{1,0:T(8,128)(2,1)}, bf16[384,2048]{1,0:T(8,128)(2,1)}, u32[]{:S(2)}, u32[]{:S(2)}) collective-permute-start(bf16[384,2048]{1,0:T(8,128)(2,1)} %split.153), channel_id=1, source_target_pairs={{0,2},{1,3},{2,0},{3,1},{4,6},{5,7},{6,4},{7,5},{8,10},{9,11},{10,... | collective-permute-start | bytes 4718600 | tf_op jit(solution)/shard_map/ppermute | solution.py:344
  605.8 52.9 %collective-permute-start.39 = (bf16[384,2048]{1,0:T(8,128)(2,1)}, bf16[384,2048]{1,0:T(8,128)(2,1)}, u32[]{:S(2)}, u32[]{:S(2)}) collective-permute-start(bf16[384,2048]{1,0:T(8,128)(2,1)} %fusion.4), channel_id=1, source_target_pairs={{0,1},{1,0},{2,3},{3,2},{4,5},{5,4},{6,7},{7,6},{8,9},{9,8},{10,11... | collective-permute-start | bytes 4718600 | tf_op jit(solution)/shard_map/ppermute | solution.py:344
  662.7 66.9 %collective-permute-start.41 = (bf16[4,256,1024]{2,1,0:T(8,128)(2,1)}, bf16[4,256,1024]{2,1,0:T(8,128)(2,1)}, u32[]{:S(2)}, u32[]{:S(2)}) collective-permute-start(bf16[4,256,1024]{2,1,0:T(8,128)(2,1)} %get-tuple-element.78), channel_id=1, source_target_pairs={{0,4},{1,5},{2,6},{3,7},{4,0},{5,1},{6,2},{7,3},{8,12},{9,13},{10,... | collective-permute-start | bytes 6291464 | tf_op jit(solution)/shard_map/ppermute | solution.py:344
  663.0 29.3 %collective-permute-start.40 = (bf16[2,256,1024]{2,1,0:T(8,128)(2,1)S(1)}, bf16[2,256,1024]{2,1,0:T(8,128)(2,1)S(1)}, u32[]{:S(2)}, u32[]{:S(2)}) collective-permute-start(bf16[2,256,1024]{2,1,0:T(8,128)(2,1)S(1)} %fusion.11), channel_id=1, source_target_pairs={{0,8},{1,9},{2,10},{3,11},{4,12},{5,13},{6,14},{7,15},{8,0},{9,1},... | collective-permute-start | bytes 3145736 | tf_op jit(solution)/shard_map/ppermute | solution.py:344
  669.2 23.1 %collective-permute-start.42 = (f32[8,896]{1,0:T(8,128)S(1)}, f32[8,896]{1,0:T(8,128)S(1)}, u32[]{:S(2)}, u32[]{:S(2)}) collective-permute-start(f32[8,896]{1,0:T(8,128)S(1)} %get-tuple-element.141), channel_id=1, source_target_pairs={{0,8},{1,9},{2,10},{3,11},{4,12},{5,13},{6,14},{7,15},{8,0},{9,1},... | collective-permute-start | bytes 86024 | tf_op jit(solution)/shard_map/ppermute | solution.py:344
  670.2 22.1 %collective-permute-start.43 = (f32[8,896]{1,0:T(8,128)S(1)}, f32[8,896]{1,0:T(8,128)S(1)}, u32[]{:S(2)}, u32[]{:S(2)}) collective-permute-start(f32[8,896]{1,0:T(8,128)S(1)} %get-tuple-element.143), channel_id=1, source_target_pairs={{0,16},{1,17},{2,18},{3,19},{4,20},{5,21},{6,22},{7,23},{8,24},{9,... | collective-permute-start | bytes 86024 | tf_op jit(solution)/shard_map/ppermute | solution.py:344
  694.0 41.5 %collective-permute-start.45 = (bf16[64,1408]{1,0:T(8,128)(2,1)S(1)}, bf16[64,1408]{1,0:T(8,128)(2,1)S(1)}, u32[]{:S(2)}, u32[]{:S(2)}) collective-permute-start(bf16[64,1408]{1,0:T(8,128)(2,1)S(1)} %get-tuple-element.127), channel_id=1, source_target_pairs={{0,1},{1,0},{2,3},{3,2},{4,5},{5,4},{6,7},{7,6},{8,9},{9,8},{10,11... | collective-permute-start | bytes 540680 | tf_op jit(solution)/shard_map/ppermute | solution.py:344
  694.4 41.1 %collective-permute-start.46 = (bf16[64,1408]{1,0:T(8,128)(2,1)S(1)}, bf16[64,1408]{1,0:T(8,128)(2,1)S(1)}, u32[]{:S(2)}, u32[]{:S(2)}) collective-permute-start(bf16[64,1408]{1,0:T(8,128)(2,1)S(1)} %get-tuple-element.126), channel_id=1, source_target_pairs={{0,2},{1,3},{2,0},{3,1},{4,6},{5,7},{6,4},{7,5},{8,10},{9,11},{10,... | collective-permute-start | bytes 540680 | tf_op jit(solution)/shard_map/ppermute | solution.py:344
  701.9 33.7 %collective-permute-start.47 = (bf16[64,1408]{1,0:T(8,128)(2,1)S(1)}, bf16[64,1408]{1,0:T(8,128)(2,1)S(1)}, u32[]{:S(2)}, u32[]{:S(2)}) collective-permute-start(bf16[64,1408]{1,0:T(8,128)(2,1)S(1)} %get-tuple-element.125), channel_id=1, source_target_pairs={{0,3},{1,2},{2,1},{3,0},{4,7},{5,6},{6,5},{7,4},{8,11},{9,10},{10,... | collective-permute-start | bytes 540680 | tf_op jit(solution)/shard_map/ppermute | solution.py:344
  743.7 38.2 %collective-permute-start.52 = (bf16[2,256,1024]{2,1,0:T(8,128)(2,1)}, bf16[2,256,1024]{2,1,0:T(8,128)(2,1)}, u32[]{:S(2)}, u32[]{:S(2)}) collective-permute-start(bf16[2,256,1024]{2,1,0:T(8,128)(2,1)} %fusion.12), channel_id=1, source_target_pairs={{0,8},{1,9},{2,10},{3,11},{4,12},{5,13},{6,14},{7,15},{8,0},{9,1},... | collective-permute-start | bytes 3145736 | tf_op jit(solution)/shard_map/ppermute | solution.py:344
  745.6 35.1 %collective-permute-start.51 = (bf16[1,256,1024]{2,1,0:T(8,128)(2,1)S(1)}, bf16[1,256,1024]{2,1,0:T(8,128)(2,1)}, u32[]{:S(2)}, u32[]{:S(2)}) collective-permute-start(bf16[1,256,1024]{2,1,0:T(8,128)(2,1)S(1)} %dynamic-slice_convert_fusion.1), channel_id=1, source_target_pairs={{0,16},{1,17},{2,18},{3,19},{4,20},{5,21},{6,22},{7,23},{8,24},{9,... | collective-permute-start | bytes 1572872 | tf_op jit(solution)/shard_map/ppermute | solution.py:344
  750.5 59.1 %collective-permute-start.49 = (bf16[384,2048]{1,0:T(8,128)(2,1)}, bf16[384,2048]{1,0:T(8,128)(2,1)}, u32[]{:S(2)}, u32[]{:S(2)}) collective-permute-start(bf16[384,2048]{1,0:T(8,128)(2,1)} %split.150), channel_id=1, source_target_pairs={{0,2},{1,3},{2,0},{3,1},{4,6},{5,7},{6,4},{7,5},{8,10},{9,11},{10,... | collective-permute-start | bytes 4718600 | tf_op jit(solution)/shard_map/ppermute | solution.py:344
  792.5 75.5 %collective-permute-start.48 = (bf16[384,2048]{1,0:T(8,128)(2,1)}, bf16[384,2048]{1,0:T(8,128)(2,1)}, u32[]{:S(2)}, u32[]{:S(2)}) collective-permute-start(bf16[384,2048]{1,0:T(8,128)(2,1)} %split.151), channel_id=1, source_target_pairs={{0,2},{1,3},{2,0},{3,1},{4,6},{5,7},{6,4},{7,5},{8,10},{9,11},{10,... | collective-permute-start | bytes 4718600 | tf_op jit(solution)/shard_map/ppermute | solution.py:344
  805.5 22.3 %collective-permute-start.56 = (bf16[1,256,1024]{2,1,0:T(8,128)(2,1)S(1)}, bf16[1,256,1024]{2,1,0:T(8,128)(2,1)}, u32[]{:S(2)}, u32[]{:S(2)}) collective-permute-start(bf16[1,256,1024]{2,1,0:T(8,128)(2,1)S(1)} %dynamic-slice_convert_fusion), channel_id=1, source_target_pairs={{0,16},{1,17},{2,18},{3,19},{4,20},{5,21},{6,22},{7,23},{8,24},{9,... | collective-permute-start | bytes 1572872 | tf_op jit(solution)/shard_map/ppermute | solution.py:344
  813.6 54.4 %collective-permute-start.50 = (bf16[384,2048]{1,0:T(8,128)(2,1)}, bf16[384,2048]{1,0:T(8,128)(2,1)}, u32[]{:S(2)}, u32[]{:S(2)}) collective-permute-start(bf16[384,2048]{1,0:T(8,128)(2,1)} %add_convert_fusion.1), channel_id=1, source_target_pairs={{0,1},{1,0},{2,3},{3,2},{4,5},{5,4},{6,7},{7,6},{8,9},{9,8},{10,11... | collective-permute-start | bytes 4718600 | tf_op jit(solution)/shard_map/ppermute | solution.py:344
  832.1 22.6 %collective-permute-start.61 = (bf16[64,512]{1,0:T(8,128)(2,1)S(1)}, bf16[64,512]{1,0:T(8,128)(2,1)S(1)}, u32[]{:S(2)}, u32[]{:S(2)}) collective-permute-start(bf16[64,512]{1,0:T(8,128)(2,1)S(1)} %bitcast.197), channel_id=1, source_target_pairs={{0,2},{1,3},{2,0},{3,1},{4,6},{5,7},{6,4},{7,5},{8,10},{9,11},{10,... | collective-permute-start | bytes 196616 | tf_op jit(solution)/shard_map/ppermute | solution.py:344
  (105 other events, 820.1 us)
Sparse Core Ops, SparseCore 0:
  23.6 125.0 all-gather.6
  150.9 161.8 all-gather.10
  315.0 90.7 all-gather.8
  409.3 110.2 reduce-scatter.4
  523.0 217.8 reduce-scatter.2

commit v2 on v1

--- a/solution.py
+++ b/solution.py
@@ -688,9 +688,12 @@
             for pair in range(narrow)
         ]
         down_got = layout.swap_group(down_sum.reshape(group, share, units), member)
-        return small_line, token_grad, mixed_parts, gate_up_sum, down_got
-
-    qkv_sum, out_sum, (small_line, token_grad, mixed_parts, gate_up_sum, down_got) = scatter_attention(
+        down_grad = jnp.transpose(
+            down_got.reshape(group, share, outer // 2, unit_rows), (1, 2, 0, 3)
+        ).reshape(share, FF)
+        return small_line, token_grad, mixed_parts, gate_up_sum, down_grad
+
+    qkv_sum, out_sum, (small_line, token_grad, mixed_parts, gate_up_sum, down_grad) = scatter_attention(
         layout, grad_proj, in_group, grad_attn, attended, qkv_weight.shape[0], place, input_grad, meanwhile
     )
     mixed_sums = layout.across_cores(mixed_parts)
@@ -699,9 +702,6 @@
 
     if heads_dealt(layout, qkv_weight.shape[0]):
         qkv_sum = deal_back(layout, qkv_sum, member)
-    down_grad = jnp.transpose(
-        down_got.reshape(group, share, outer // 2, unit_rows), (1, 2, 0, 3)
-    ).reshape(share, FF)
     out_got = layout.swap_group(out_sum.reshape(group, share, head_cols), member)
     out_grad = jnp.transpose(
         out_got.reshape(group, share, H // group, HD), (1, 2, 0, 3)

time: 887 us -> 881 us (level)
    convert_element_type x3 -> x0, local copies, waits for them, and re-layouts: 9.3 us -> none  [per_device(): down_grad.astype(F32)]
  transfers between devices with their start and end apart: 68 -> 68, of which waited for: 31 -> 30; matrix products, arithmetic and copies ran while one was open for 32% -> 32% of each run, Pallas kernels for 13% -> 13%
where the time goes in v2:
time: 881 us; the launch traced here: 873 us
  waiting for transfers between devices  373 us (42%)
  matrix products  125 us (14%)
  Pallas kernels  116 us (13%)
  other arithmetic  91.8 us (10%)
  local copies, waits for them, and re-layouts  86 us (10%)
  starting transfers between devices  65.7 us (7%)
  between operations  15.7 us (2%)
    ppermute x57, waiting for transfers between devices, swap(): return lax.ppermute(value, AXES, [(i, i ^ mask) for i in range(self.count)])  312 us
    ppermute x57, starting transfers between devices, swap(): return lax.ppermute(value, AXES, [(i, i ^ mask) for i in range(self.count)])  53.4 us
    all_gather x3, waiting for transfers between devices, gather_outer(): lax.all_gather(value, AXES, axis=0, axis_index_groups=self.outer_groups)  53.4 us
    dot_general x2, matrix products, weight_grad(): lax.dot_general(grad_rows, inputs, (((0,), (0,)), ((), ())), preferred_el...  37.8 us
    pallas_call x4, Pallas kernels, rows_product(): pl.pallas_call(kernel, grid=(cols // width,), in_specs=[pl.BlockSpec((cou...  36.3 us
    dot_general x3, matrix products, mul_rows(): lax.dot_general(left, weight, (((1,), (1,)), ((), ())), preferred_element...  35.3 us
    pallas_call x1, Pallas kernels, attend(): pl.pallas_call(attend_kernel, grid=(steps, rows // count_tok), in_specs=[...  29.8 us
    pallas_call x2, Pallas kernels, attention_grads(): pl.pallas_call(kernel, grid_spec=pltpu.PrefetchScalarGridSpec(num_scalar_...  26.6 us
  transfers between devices with their start and end apart: 68, of which 30 were waited for; matrix products, arithmetic and copies ran while one was open for 32% of the time, Pallas kernels for 13%

profile of v2, /device:TPU:13, one launch (start us, length us, event | category | flops | bytes accessed | tf_op | source)
XLA Modules:
  0.0 873.1 jit_solution(7458198394612910678)
XLA Ops:
  15.3 6.9 collective-permute-done.13
  47.9 30.4 %collective-permute-done.7 = bf16[384,2048]{1,0:T(8,128)(2,1)} collective-permute-done((bf16[384,2048]{1,0:T(8,128)(2,1)}, bf16[384,2048]{1,0:T(8,128)(2,1)}, u32[]{:S(2)}, u32[]{:S(2)}) %collective-permute-start.7) | collective-permute-done | bytes 1572896 | tf_op jit(solution)/shard_map/ppermute | solution.py:344
  100.5 33.4 %collective-permute-done.19 = s32[1,384]{1,0:T(1,128)S(1)} collective-permute-done((s32[1,384]{1,0:T(1,128)S(1)}, s32[1,384]{1,0:T(1,128)S(1)}, u32[]{:S(2)}, u32[]{:S(2)}) %collective-permute-start.19) | collective-permute-done | bytes 1568 | tf_op jit(solution)/shard_map/ppermute | solution.py:344
  161.0 7.1 slice.151
  168.1 29.8 %attend.1 = (bf16[1536,512]{1,0:T(8,128)(2,1)S(1)}, bf16[1536,512]{1,0:T(8,128)(2,1)S(1)}, bf16[1536,512]{1,0:T(8,128)(2,1)S(1)}, bf16[1536,512]{1,0:T(8,128)(2,1)}) custom-call(bf16[1536,2048]{1,0:T(8,128)(2,1)} %pad_maximum_fusion.2.x_ref.input_ref, bf16[1536,2048]{1,0:T(8,128)(2,1)} %bitcast.156, bf16[1536,2048]{1,0:T(8,128)(2,1)} %bitcast.157, ...), custom_call_target="tpu_custom_call" | custom-call | flops 1 | bytes 1 | tf_op jit(solution)/shard_map/attend/pallas_call | solution.py:187
  220.4 35.0 %collective-permute-done.26 = bf16[384,2048]{1,0:T(8,128)(2,1)} collective-permute-done((bf16[384,2048]{1,0:T(8,128)(2,1)}, bf16[384,2048]{1,0:T(8,128)(2,1)}, u32[]{:S(2)}, u32[]{:S(2)}) %collective-permute-start.26) | collective-permute-done | bytes 1572896 | tf_op jit(solution)/shard_map/ppermute | solution.py:344
  263.9 33.4 %collective-permute-done.28 = bf16[384,2048]{1,0:T(8,128)(2,1)} collective-permute-done((bf16[384,2048]{1,0:T(8,128)(2,1)}, bf16[384,2048]{1,0:T(8,128)(2,1)}, u32[]{:S(2)}, u32[]{:S(2)}) %collective-permute-start.28) | collective-permute-done | bytes 1572896 | tf_op jit(solution)/shard_map/ppermute | solution.py:344
  299.4 13.4 %all-gather.11.cloned.1.call-done = bf16[2816,2048]{1,0:T(8,128)(2,1)} async-done(((bf16[352,2048]{1,0:T(8,128)(2,1)}), bf16[2816,2048]{1,0:T(8,128)(2,1)}) %all-gather.11.cloned.1.call-update) | async-done | bytes 11534352 | tf_op jit(solution)/shard_map/all_gather | solution.py:379
  312.8 29.7 %fusion.10 = f32[1536,2816]{1,0:T(8,128)} fusion(bf16[2816,2048]{1,0:T(8,128)(2,1)} %all-gather.11.cloned.1.call-done, bf16[384,2048]{1,0:T(8,128)(2,1)} %collective-permute-done.29, bf16[384,2048]{1,0:T(8,128)(2,1)} %collective-permute-done.28, bf16[384,2048]{1,0:T(8,128)(2,1)} %collective-permute-done.27, bf16[384,2048]{1,0:T(8,128)(2,1)} %add_convert_fusion.3), kind=kOutput, calls=%fused_computation.74 | convolution fusion | flops 17741905920 | bytes 35127296 | tf_op jit(solution)/shard_map/dot_general | solution.py:66
  342.5 7.2 multiply_convert_fusion.2.left_ref
  349.8 13.9 %convolution_convert_fusion.1 = bf16[2048,1408]{1,0:T(8,128)(2,1)} fusion(bf16[1536,2048]{1,0:T(8,128)(2,1)} %pad_maximum_fusion.3, bf16[1536,1408]{1,0:T(8,128)(2,1)S(1)} %multiply_convert_fusion.2.left_ref), kind=kOutput, calls=%fused_computation.12 | convolution fusion | flops 8861253632 | bytes 16384000 | tf_op jit(solution)/shard_map/dot_general | solution.py:70
  365.9 39.9 %all-gather.9.cloned.1.call-done.right_ref = bf16[2048,1408]{1,0:T(8,128)(2,1)} async-done(((bf16[256,1408]{1,0:T(8,128)(2,1)}), bf16[2048,1408]{1,0:T(8,128)(2,1)}) %all-gather.9.cloned.1.call-update) | async-done | bytes 5767184 | tf_op jit(solution)/shard_map/all_gather | solution.py:379
  405.9 21.1 %multiply_convert_fusion = (bf16[1536,1408]{1,0:T(8,128)(2,1)S(1)}, bf16[1536,1408]{1,0:T(8,128)(2,1)}) fusion(f32[1536,2816]{1,0:T(8,128)} %fusion.10, bf16[1536,2048]{1,0:T(8,128)(2,1)} %pad_maximum_fusion.3, bf16[2048,1408]{1,0:T(8,128)(2,1)} %all-gather.9.cloned.1.call-done.right_ref), kind=kOutput, calls=%fused_computation.7 | convolution fusion | flops 8884322304 | bytes 38010880 | tf_op jit(solution)/shard_map/dot_general | solution.py:619
  431.1 12.0 %fusion.2 = f32[768,2048]{1,0:T(8,128)S(1)} fusion(bf16[2816,2048]{1,0:T(8,128)(2,1)} %all-gather.11.cloned.1.call-done, bf16[1536,1408]{1,0:T(8,128)(2,1)S(1)} %copy-done.23, bf16[1536,1408]{1,0:T(8,128)(2,1)S(1)} %get-tuple-element.113), kind=kOutput, calls=%fused_computation.18 | convolution fusion | flops 8867020800 | bytes 26476544 | tf_op jit(solution)/shard_map/dot_general | solution.py:627
  450.1 23.8 %convolution_convert_fusion = bf16[2816,2048]{1,0:T(8,128)(2,1)} fusion(bf16[1536,1408]{1,0:T(8,128)(2,1)S(1)} %get-tuple-element.113, bf16[1536,1408]{1,0:T(8,128)(2,1)} %get-tuple-element.114, bf16[384,2048]{1,0:T(8,128)(2,1)} %collective-permute-done.29, bf16[384,2048]{1,0:T(8,128)(2,1)} %collective-permute-done.28, ...), kind=kOutput, calls=%fused_computation | convolution fusion | flops 17764974592 | bytes 26476544 | tf_op jit(solution)/shard_map/dot_general | solution.py:70
  473.9 11.8 %collective-permute-done.32 = bf16[384,2048]{1,0:T(8,128)(2,1)} collective-permute-done((bf16[384,2048]{1,0:T(8,128)(2,1)}, bf16[384,2048]{1,0:T(8,128)(2,1)}, u32[]{:S(2)}, u32[]{:S(2)}) %collective-permute-start.32) | collective-permute-done | bytes 1572896 | tf_op jit(solution)/shard_map/ppermute | solution.py:344
  485.8 13.2 %fusion.53 = f32[768,2048]{1,0:T(8,128)S(1)} fusion(bf16[768,2816]{1,0:T(8,128)(2,1)} %fusion, bf16[2816,2048]{1,0:T(8,128)(2,1)} %all-gather.11.cloned.1.call-done), kind=kOutput, calls=%fused_computation.225 | convolution fusion | flops 8858370048 | bytes 22151168 | tf_op jit(solution)/shard_map/dot_general | solution.py:627
  515.0 11.7 %attend_back.2.rest_0_ = bf16[1536,1536]{1,0:T(8,128)(2,1)} custom-call(bf16[1536,512]{1,0:T(8,128)(2,1)S(1)} %get-tuple-element.57.q_ref, bf16[1536,512]{1,0:T(8,128)(2,1)S(1)} %copy-done.3, bf16[1536,512]{1,0:T(8,128)(2,1)} %copy-done.5, bf16[768,512]{1,0:T(8,128)(2,1)S(1)} %convolution_convert_fusion.3.g_ref, f32[1536,256]{1,0:T(8,128)} %pad_maximum_fusion.6.cos_ref, ...), custom_call_target="tpu_custom_call" | custom-call | flops 1 | bytes 1 | tf_op jit(solution)/shard_map/attend_back/pallas_call | solution.py:226
  528.8 17.3 %collective-permute-done.33 = bf16[384,2048]{1,0:T(8,128)(2,1)} collective-permute-done((bf16[384,2048]{1,0:T(8,128)(2,1)S(1)}, bf16[384,2048]{1,0:T(8,128)(2,1)}, u32[]{:S(2)}, u32[]{:S(2)}) %collective-permute-start.33) | collective-permute-done | bytes 1572896 | tf_op jit(solution)/shard_map/ppermute | solution.py:344
  554.6 11.6 %attend_back.3.proj_ref.left_ref = bf16[1536,1536]{1,0:T(8,128)(2,1)} custom-call(bf16[1536,512]{1,0:T(8,128)(2,1)S(1)} %get-tuple-element.57.q_ref, bf16[1536,512]{1,0:T(8,128)(2,1)S(1)} %copy-done.4, bf16[1536,512]{1,0:T(8,128)(2,1)} %copy-done.5, bf16[768,512]{1,0:T(8,128)(2,1)S(1)} %convolution_convert_fusion.2.g_ref, ...), custom_call_target="tpu_custom_call", output_to_operand_aliasing={{}: (9, {})} | custom-call | flops 1 | bytes 1 | tf_op jit(solution)/shard_map/attend_back/pallas_call | solution.py:226
  566.2 13.2 %attention_grads.2 = (bf16[4,256,1024]{2,1,0:T(8,128)(2,1)}, f32[4,256,1024]{2,1,0:T(8,128)}) custom-call(s32[1]{0:T(128)} %bitcast.46.side_ref, bf16[1536,1536]{1,0:T(8,128)(2,1)} %attend_back.3.proj_ref.left_ref, bf16[1536,2048]{1,0:T(8,128)(2,1)} %pad_maximum_fusion.2.x_ref.input_ref, bf16[1536,512]{1,0:T(8,128)(2,1)} %get-tuple-element.56.attended_ref, ...), custom_call_target="tpu_custom_call" | custom-call | flops 1 | bytes 1 | tf_op jit(solution)/shard_map/attention_grads/pallas_call | solution.py:305
  579.4 9.1 %rows_product.5 = f32[768,2048]{1,0:T(8,128)} custom-call(bf16[1536,1536]{1,0:T(8,128)(2,1)S(1)} %bitcast.152, bf16[1536,2048]{1,0:T(8,128)(2,1)} %bitcast.159), custom_call_target="tpu_custom_call" | custom-call | flops 1 | bytes 1 | tf_op jit(solution)/shard_map/rows_product/pallas_call | solution.py:254
  591.4 9.0 %rows_product.4 = f32[768,2048]{1,0:T(8,128)} custom-call(bf16[1536,1536]{1,0:T(8,128)(2,1)S(1)} %bitcast.152, bf16[1536,2048]{1,0:T(8,128)(2,1)} %bitcast.160), custom_call_target="tpu_custom_call" | custom-call | flops 1 | bytes 1 | tf_op jit(solution)/shard_map/rows_product/pallas_call | solution.py:254
  606.2 13.4 %attention_grads.3 = (bf16[4,256,1024]{2,1,0:T(8,128)(2,1)}, f32[4,256,1024]{2,1,0:T(8,128)}) custom-call(s32[1]{0:T(128)} %bitcast.46.side_ref, bf16[1536,1536]{1,0:T(8,128)(2,1)} %attend_back.3.proj_ref.left_ref, bf16[1536,2048]{1,0:T(8,128)(2,1)} %pad_maximum_fusion.2.x_ref.input_ref, bf16[1536,512]{1,0:T(8,128)(2,1)} %get-tuple-element.56.attended_ref, ...), custom_call_target="tpu_custom_call" | custom-call | flops 1 | bytes 1 | tf_op jit(solution)/shard_map/attention_grads/pallas_call | solution.py:305
  620.6 34.3 %collective-permute-done.36 = bf16[4,256,1024]{2,1,0:T(8,128)(2,1)} collective-permute-done((bf16[4,256,1024]{2,1,0:T(8,128)(2,1)}, bf16[4,256,1024]{2,1,0:T(8,128)(2,1)}, u32[]{:S(2)}, u32[]{:S(2)}) %collective-permute-start.36) | collective-permute-done | bytes 2097184 | tf_op jit(solution)/shard_map/ppermute | solution.py:344
  674.2 9.1 %rows_product.7 = f32[768,2048]{1,0:T(8,128)} custom-call(bf16[1536,1408]{1,0:T(8,128)(2,1)S(1)} %copy-done.1, bf16[2048,1408]{1,0:T(8,128)(2,1)} %all-gather.9.cloned.1.call-done.right_ref), custom_call_target="tpu_custom_call" | custom-call | flops 1 | bytes 1 | tf_op jit(solution)/shard_map/rows_product/pallas_call | solution.py:254
  683.3 9.0 %rows_product.6 = f32[768,2048]{1,0:T(8,128)} custom-call(bf16[1536,1408]{1,0:T(8,128)(2,1)S(1)} %copy-done.1, bf16[2048,1408]{1,0:T(8,128)(2,1)} %all-gather.9.cloned.1.call-done.right_ref), custom_call_target="tpu_custom_call" | custom-call | flops 1 | bytes 1 | tf_op jit(solution)/shard_map/rows_product/pallas_call | solution.py:254
  695.9 7.3 collective-permute-start.46
  704.1 25.4 %collective-permute-done.41 = bf16[4,256,1024]{2,1,0:T(8,128)(2,1)} collective-permute-done((bf16[4,256,1024]{2,1,0:T(8,128)(2,1)}, bf16[4,256,1024]{2,1,0:T(8,128)(2,1)}, u32[]{:S(2)}, u32[]{:S(2)}) %collective-permute-start.41) | collective-permute-done | bytes 2097184 | tf_op jit(solution)/shard_map/ppermute | solution.py:344
  755.1 27.9 %collective-permute-done.51 = bf16[1,256,1024]{2,1,0:T(8,128)(2,1)} collective-permute-done((bf16[1,256,1024]{2,1,0:T(8,128)(2,1)S(1)}, bf16[1,256,1024]{2,1,0:T(8,128)(2,1)}, u32[]{:S(2)}, u32[]{:S(2)}) %collective-permute-start.51) | collective-permute-done | bytes 524320 | tf_op jit(solution)/shard_map/ppermute | solution.py:344
  807.2 13.8 %collective-permute-done.56 = bf16[1,256,1024]{2,1,0:T(8,128)(2,1)} collective-permute-done((bf16[1,256,1024]{2,1,0:T(8,128)(2,1)S(1)}, bf16[1,256,1024]{2,1,0:T(8,128)(2,1)}, u32[]{:S(2)}, u32[]{:S(2)}) %collective-permute-start.56) | collective-permute-done | bytes 524320 | tf_op jit(solution)/shard_map/ppermute | solution.py:344
  827.3 15.7 %collective-permute-done.60 = bf16[64,512]{1,0:T(8,128)(2,1)S(1)} collective-permute-done((bf16[64,512]{1,0:T(8,128)(2,1)S(1)}, bf16[64,512]{1,0:T(8,128)(2,1)S(1)}, u32[]{:S(2)}, u32[]{:S(2)}) %collective-permute-start.60) | collective-permute-done | bytes 65568 | tf_op jit(solution)/shard_map/ppermute | solution.py:344
  (468 shorter events, 267.3 us)
Async XLA Ops:
  7.2 153.8 %all-gather.7.cloned.1.call-start = ((), (), s32[]{:S(2)}) async-start(), calls=%async_computation.4 | async-start | bytes 9437184 | tf_op jit(solution)/shard_map/all_gather | solution.py:379
  23.5 289.3 %all-gather.11.cloned.1.call-start = ((), (), s32[]{:S(2)}) async-start(), calls=%async_computation.6 | async-start | bytes 12976128 | tf_op jit(solution)/shard_map/all_gather | solution.py:379
  24.2 381.6 %all-gather.9.cloned.1.call-start = ((), (), s32[]{:S(2)}) async-start(), calls=%async_computation.5 | async-start | bytes 6488064 | tf_op jit(solution)/shard_map/all_gather | solution.py:379
  43.7 34.5 %collective-permute-start.7 = (bf16[384,2048]{1,0:T(8,128)(2,1)}, bf16[384,2048]{1,0:T(8,128)(2,1)}, u32[]{:S(2)}, u32[]{:S(2)}) collective-permute-start(bf16[384,2048]{1,0:T(8,128)(2,1)} %add_convert_fusion.4), channel_id=1, source_target_pairs={{0,1},{1,0},{2,3},{3,2},{4,5},{5,4},{6,7},{7,6},{8,9},{9,8},{10,11... | collective-permute-start | bytes 4718600 | tf_op jit(solution)/shard_map/ppermute | solution.py:344
  45.8 45.8 %collective-permute-start.6 = (bf16[384,2048]{1,0:T(8,128)(2,1)}, bf16[384,2048]{1,0:T(8,128)(2,1)S(1)}, u32[]{:S(2)}, u32[]{:S(2)}) collective-permute-start(bf16[384,2048]{1,0:T(8,128)(2,1)} %add_convert_fusion.4), channel_id=1, source_target_pairs={{0,2},{1,3},{2,0},{3,1},{4,6},{5,7},{6,4},{7,5},{8,10},{9,11},{10,... | collective-permute-start | bytes 4718600 | tf_op jit(solution)/shard_map/ppermute | solution.py:344
  97.6 38.5 %collective-permute-start.22 = (bf16[384,2048]{1,0:T(8,128)(2,1)S(1)}, bf16[384,2048]{1,0:T(8,128)(2,1)}, u32[]{:S(2)}, u32[]{:S(2)}) collective-permute-start(bf16[384,2048]{1,0:T(8,128)(2,1)S(1)} %copy-done.21), channel_id=1, source_target_pairs={{0,1},{1,0},{2,3},{3,2},{4,5},{5,4},{6,7},{7,6},{8,9},{9,8},{10,11... | collective-permute-start | bytes 4718600 | tf_op jit(solution)/shard_map/ppermute | solution.py:344
  97.7 36.3 %collective-permute-start.19 = (s32[1,384]{1,0:T(1,128)S(1)}, s32[1,384]{1,0:T(1,128)S(1)}, u32[]{:S(2)}, u32[]{:S(2)}) collective-permute-start(s32[1,384]{1,0:T(1,128)S(1)} %copy-done.54), channel_id=1, source_target_pairs={{0,1},{1,0},{2,3},{3,2},{4,5},{5,4},{6,7},{7,6},{8,9},{9,8},{10,11... | collective-permute-start | bytes 4616 | tf_op jit(solution)/shard_map/ppermute | solution.py:344
  99.1 35.5 %collective-permute-start.18 = (s32[1,384]{1,0:T(1,128)S(1)}, s32[1,384]{1,0:T(1,128)S(1)}, u32[]{:S(2)}, u32[]{:S(2)}) collective-permute-start(s32[1,384]{1,0:T(1,128)S(1)} %copy-done.54), channel_id=1, source_target_pairs={{0,2},{1,3},{2,0},{3,1},{4,6},{5,7},{6,4},{7,5},{8,10},{9,11},{10,... | collective-permute-start | bytes 4616 | tf_op jit(solution)/shard_map/ppermute | solution.py:344
  219.5 35.9 %collective-permute-start.26 = (bf16[384,2048]{1,0:T(8,128)(2,1)}, bf16[384,2048]{1,0:T(8,128)(2,1)}, u32[]{:S(2)}, u32[]{:S(2)}) collective-permute-start(bf16[384,2048]{1,0:T(8,128)(2,1)} %fusion.7), channel_id=1, source_target_pairs={{0,1},{1,0},{2,3},{3,2},{4,5},{5,4},{6,7},{7,6},{8,9},{9,8},{10,11... | collective-permute-start | bytes 4718600 | tf_op jit(solution)/shard_map/ppermute | solution.py:344
  262.2 35.1 %collective-permute-start.28 = (bf16[384,2048]{1,0:T(8,128)(2,1)}, bf16[384,2048]{1,0:T(8,128)(2,1)}, u32[]{:S(2)}, u32[]{:S(2)}) collective-permute-start(bf16[384,2048]{1,0:T(8,128)(2,1)} %add_convert_fusion.3), channel_id=1, source_target_pairs={{0,1},{1,0},{2,3},{3,2},{4,5},{5,4},{6,7},{7,6},{8,9},{9,8},{10,11... | collective-permute-start | bytes 4718600 | tf_op jit(solution)/shard_map/ppermute | solution.py:344
  262.3 430.5 %reduce-scatter.5.cloned.1.call-start = ((), (), s32[]{:S(2)}) async-start(), calls=%async_computation.3 | async-start | bytes 6488064 | tf_op jit(solution)/shard_map/reduce_scatter | solution.py:382
  262.3 37.0 %collective-permute-start.27 = (bf16[384,2048]{1,0:T(8,128)(2,1)}, bf16[384,2048]{1,0:T(8,128)(2,1)}, u32[]{:S(2)}, u32[]{:S(2)}) collective-permute-start(bf16[384,2048]{1,0:T(8,128)(2,1)} %add_convert_fusion.3), channel_id=1, source_target_pairs={{0,2},{1,3},{2,0},{3,1},{4,6},{5,7},{6,4},{7,5},{8,10},{9,11},{10,... | collective-permute-start | bytes 4718600 | tf_op jit(solution)/shard_map/ppermute | solution.py:344
  405.8 338.4 %reduce-scatter.3.cloned.1.call-start = ((), (), s32[]{:S(2)}) async-start(), calls=%async_computation.2 | async-start | bytes 12976128 | tf_op jit(solution)/shard_map/reduce_scatter | solution.py:382
  449.8 35.9 %collective-permute-start.32 = (bf16[384,2048]{1,0:T(8,128)(2,1)}, bf16[384,2048]{1,0:T(8,128)(2,1)}, u32[]{:S(2)}, u32[]{:S(2)}) collective-permute-start(bf16[384,2048]{1,0:T(8,128)(2,1)} %add_convert_fusion.2), channel_id=1, source_target_pairs={{0,1},{1,0},{2,3},{3,2},{4,5},{5,4},{6,7},{7,6},{8,9},{9,8},{10,11... | collective-permute-start | bytes 4718600 | tf_op jit(solution)/shard_map/ppermute | solution.py:344
  510.1 35.9 %collective-permute-start.33 = (bf16[384,2048]{1,0:T(8,128)(2,1)S(1)}, bf16[384,2048]{1,0:T(8,128)(2,1)}, u32[]{:S(2)}, u32[]{:S(2)}) collective-permute-start(bf16[384,2048]{1,0:T(8,128)(2,1)S(1)} %get-tuple-element.108), channel_id=1, source_target_pairs={{0,1},{1,0},{2,3},{3,2},{4,5},{5,4},{6,7},{7,6},{8,9},{9,8},{10,11... | collective-permute-start | bytes 4718600 | tf_op jit(solution)/shard_map/ppermute | solution.py:344
  591.2 63.7 %collective-permute-start.36 = (bf16[4,256,1024]{2,1,0:T(8,128)(2,1)}, bf16[4,256,1024]{2,1,0:T(8,128)(2,1)}, u32[]{:S(2)}, u32[]{:S(2)}) collective-permute-start(bf16[4,256,1024]{2,1,0:T(8,128)(2,1)} %get-tuple-element.72), channel_id=1, source_target_pairs={{0,4},{1,5},{2,6},{3,7},{4,0},{5,1},{6,2},{7,3},{8,12},{9,13},{10,... | collective-permute-start | bytes 6291464 | tf_op jit(solution)/shard_map/ppermute | solution.py:344
  603.7 54.9 %collective-permute-start.37 = (bf16[384,2048]{1,0:T(8,128)(2,1)}, bf16[384,2048]{1,0:T(8,128)(2,1)}, u32[]{:S(2)}, u32[]{:S(2)}) collective-permute-start(bf16[384,2048]{1,0:T(8,128)(2,1)} %split.153), channel_id=1, source_target_pairs={{0,2},{1,3},{2,0},{3,1},{4,6},{5,7},{6,4},{7,5},{8,10},{9,11},{10,... | collective-permute-start | bytes 4718600 | tf_op jit(solution)/shard_map/ppermute | solution.py:344
  605.8 52.7 %collective-permute-start.39 = (bf16[384,2048]{1,0:T(8,128)(2,1)}, bf16[384,2048]{1,0:T(8,128)(2,1)}, u32[]{:S(2)}, u32[]{:S(2)}) collective-permute-start(bf16[384,2048]{1,0:T(8,128)(2,1)} %fusion.4), channel_id=1, source_target_pairs={{0,1},{1,0},{2,3},{3,2},{4,5},{5,4},{6,7},{7,6},{8,9},{9,8},{10,11... | collective-permute-start | bytes 4718600 | tf_op jit(solution)/shard_map/ppermute | solution.py:344
  662.6 66.9 %collective-permute-start.41 = (bf16[4,256,1024]{2,1,0:T(8,128)(2,1)}, bf16[4,256,1024]{2,1,0:T(8,128)(2,1)}, u32[]{:S(2)}, u32[]{:S(2)}) collective-permute-start(bf16[4,256,1024]{2,1,0:T(8,128)(2,1)} %get-tuple-element.78), channel_id=1, source_target_pairs={{0,4},{1,5},{2,6},{3,7},{4,0},{5,1},{6,2},{7,3},{8,12},{9,13},{10,... | collective-permute-start | bytes 6291464 | tf_op jit(solution)/shard_map/ppermute | solution.py:344
  662.9 29.5 %collective-permute-start.40 = (bf16[2,256,1024]{2,1,0:T(8,128)(2,1)S(1)}, bf16[2,256,1024]{2,1,0:T(8,128)(2,1)S(1)}, u32[]{:S(2)}, u32[]{:S(2)}) collective-permute-start(bf16[2,256,1024]{2,1,0:T(8,128)(2,1)S(1)} %fusion.11), channel_id=1, source_target_pairs={{0,8},{1,9},{2,10},{3,11},{4,12},{5,13},{6,14},{7,15},{8,0},{9,1},... | collective-permute-start | bytes 3145736 | tf_op jit(solution)/shard_map/ppermute | solution.py:344
  669.3 23.1 %collective-permute-start.42 = (f32[8,896]{1,0:T(8,128)S(1)}, f32[8,896]{1,0:T(8,128)S(1)}, u32[]{:S(2)}, u32[]{:S(2)}) collective-permute-start(f32[8,896]{1,0:T(8,128)S(1)} %get-tuple-element.141), channel_id=1, source_target_pairs={{0,8},{1,9},{2,10},{3,11},{4,12},{5,13},{6,14},{7,15},{8,0},{9,1},... | collective-permute-start | bytes 86024 | tf_op jit(solution)/shard_map/ppermute | solution.py:344
  670.1 22.3 %collective-permute-start.43 = (f32[8,896]{1,0:T(8,128)S(1)}, f32[8,896]{1,0:T(8,128)S(1)}, u32[]{:S(2)}, u32[]{:S(2)}) collective-permute-start(f32[8,896]{1,0:T(8,128)S(1)} %get-tuple-element.143), channel_id=1, source_target_pairs={{0,16},{1,17},{2,18},{3,19},{4,20},{5,21},{6,22},{7,23},{8,24},{9,... | collective-permute-start | bytes 86024 | tf_op jit(solution)/shard_map/ppermute | solution.py:344
  695.6 39.9 %collective-permute-start.45 = (bf16[64,1408]{1,0:T(8,128)(2,1)S(1)}, bf16[64,1408]{1,0:T(8,128)(2,1)S(1)}, u32[]{:S(2)}, u32[]{:S(2)}) collective-permute-start(bf16[64,1408]{1,0:T(8,128)(2,1)S(1)} %get-tuple-element.127), channel_id=1, source_target_pairs={{0,1},{1,0},{2,3},{3,2},{4,5},{5,4},{6,7},{7,6},{8,9},{9,8},{10,11... | collective-permute-start | bytes 540680 | tf_op jit(solution)/shard_map/ppermute | solution.py:344
  695.9 40.2 %collective-permute-start.46 = (bf16[64,1408]{1,0:T(8,128)(2,1)S(1)}, bf16[64,1408]{1,0:T(8,128)(2,1)S(1)}, u32[]{:S(2)}, u32[]{:S(2)}) collective-permute-start(bf16[64,1408]{1,0:T(8,128)(2,1)S(1)} %get-tuple-element.126), channel_id=1, source_target_pairs={{0,2},{1,3},{2,0},{3,1},{4,6},{5,7},{6,4},{7,5},{8,10},{9,11},{10,... | collective-permute-start | bytes 540680 | tf_op jit(solution)/shard_map/ppermute | solution.py:344
  703.2 33.6 %collective-permute-start.47 = (bf16[64,1408]{1,0:T(8,128)(2,1)S(1)}, bf16[64,1408]{1,0:T(8,128)(2,1)S(1)}, u32[]{:S(2)}, u32[]{:S(2)}) collective-permute-start(bf16[64,1408]{1,0:T(8,128)(2,1)S(1)} %get-tuple-element.125), channel_id=1, source_target_pairs={{0,3},{1,2},{2,1},{3,0},{4,7},{5,6},{6,5},{7,4},{8,11},{9,10},{10,... | collective-permute-start | bytes 540680 | tf_op jit(solution)/shard_map/ppermute | solution.py:344
  746.9 37.2 %collective-permute-start.52 = (bf16[2,256,1024]{2,1,0:T(8,128)(2,1)}, bf16[2,256,1024]{2,1,0:T(8,128)(2,1)}, u32[]{:S(2)}, u32[]{:S(2)}) collective-permute-start(bf16[2,256,1024]{2,1,0:T(8,128)(2,1)} %fusion.12), channel_id=1, source_target_pairs={{0,8},{1,9},{2,10},{3,11},{4,12},{5,13},{6,14},{7,15},{8,0},{9,1},... | collective-permute-start | bytes 3145736 | tf_op jit(solution)/shard_map/ppermute | solution.py:344
  748.4 34.6 %collective-permute-start.51 = (bf16[1,256,1024]{2,1,0:T(8,128)(2,1)S(1)}, bf16[1,256,1024]{2,1,0:T(8,128)(2,1)}, u32[]{:S(2)}, u32[]{:S(2)}) collective-permute-start(bf16[1,256,1024]{2,1,0:T(8,128)(2,1)S(1)} %dynamic-slice_convert_fusion.1), channel_id=1, source_target_pairs={{0,16},{1,17},{2,18},{3,19},{4,20},{5,21},{6,22},{7,23},{8,24},{9,... | collective-permute-start | bytes 1572872 | tf_op jit(solution)/shard_map/ppermute | solution.py:344
  753.2 49.8 %collective-permute-start.49 = (bf16[384,2048]{1,0:T(8,128)(2,1)}, bf16[384,2048]{1,0:T(8,128)(2,1)}, u32[]{:S(2)}, u32[]{:S(2)}) collective-permute-start(bf16[384,2048]{1,0:T(8,128)(2,1)} %split.150), channel_id=1, source_target_pairs={{0,2},{1,3},{2,0},{3,1},{4,6},{5,7},{6,4},{7,5},{8,10},{9,11},{10,... | collective-permute-start | bytes 4718600 | tf_op jit(solution)/shard_map/ppermute | solution.py:344
  795.3 66.0 %collective-permute-start.48 = (bf16[384,2048]{1,0:T(8,128)(2,1)}, bf16[384,2048]{1,0:T(8,128)(2,1)}, u32[]{:S(2)}, u32[]{:S(2)}) collective-permute-start(bf16[384,2048]{1,0:T(8,128)(2,1)} %split.151), channel_id=1, source_target_pairs={{0,2},{1,3},{2,0},{3,1},{4,6},{5,7},{6,4},{7,5},{8,10},{9,11},{10,... | collective-permute-start | bytes 4718600 | tf_op jit(solution)/shard_map/ppermute | solution.py:344
  798.9 22.1 %collective-permute-start.56 = (bf16[1,256,1024]{2,1,0:T(8,128)(2,1)S(1)}, bf16[1,256,1024]{2,1,0:T(8,128)(2,1)}, u32[]{:S(2)}, u32[]{:S(2)}) collective-permute-start(bf16[1,256,1024]{2,1,0:T(8,128)(2,1)S(1)} %dynamic-slice_convert_fusion), channel_id=1, source_target_pairs={{0,16},{1,17},{2,18},{3,19},{4,20},{5,21},{6,22},{7,23},{8,24},{9,... | collective-permute-start | bytes 1572872 | tf_op jit(solution)/shard_map/ppermute | solution.py:344
  806.9 54.4 %collective-permute-start.50 = (bf16[384,2048]{1,0:T(8,128)(2,1)}, bf16[384,2048]{1,0:T(8,128)(2,1)}, u32[]{:S(2)}, u32[]{:S(2)}) collective-permute-start(bf16[384,2048]{1,0:T(8,128)(2,1)} %add_convert_fusion.1), channel_id=1, source_target_pairs={{0,1},{1,0},{2,3},{3,2},{4,5},{5,4},{6,7},{7,6},{8,9},{9,8},{10,11... | collective-permute-start | bytes 4718600 | tf_op jit(solution)/shard_map/ppermute | solution.py:344
  825.3 22.7 %collective-permute-start.61 = (bf16[64,512]{1,0:T(8,128)(2,1)S(1)}, bf16[64,512]{1,0:T(8,128)(2,1)S(1)}, u32[]{:S(2)}, u32[]{:S(2)}) collective-permute-start(bf16[64,512]{1,0:T(8,128)(2,1)S(1)} %bitcast.197), channel_id=1, source_target_pairs={{0,2},{1,3},{2,0},{3,1},{4,6},{5,7},{6,4},{7,5},{8,10},{9,11},{10,... | collective-permute-start | bytes 196616 | tf_op jit(solution)/shard_map/ppermute | solution.py:344
  (106 other events, 814.7 us)
Sparse Core Ops, SparseCore 0:
  23.6 125.0 all-gather.6
  150.9 161.8 all-gather.10
  315.0 90.7 all-gather.8
  409.3 110.2 reduce-scatter.4
  523.1 217.8 reduce-scatter.2
